TPU v7x, 128 devices: a whole 4x4x4 slice. The times are simulated.
128 devices in a mesh: slab: 32 (over x, z, core), gy: 4 (over y).
Axes of the slice: x: 4, y: 4, z: 4, core: 2. Of those that a mesh axis runs over, the one named last changes fastest.
Arguments:
- displacement: float32 [3, 32, 256, 512], P(None, None, 'slab', 'gy'), may hold values from -6 to 6
- previous: float32 [3, 32, 256, 512], P(None, None, 'slab', 'gy'), may hold values from -6 to 6
- shear_coef: float32 [32, 256, 512], P(None, 'slab', 'gy'), may hold values from 0.04 to 0.16
- bulk_coef: float32 [32, 256, 512], P(None, 'slab', 'gy'), may hold values from 0.02 to 0.16
- cell_index: int32 [131072], P(('slab', 'gy')), may hold values from 0 to 131071, as said below
- archetype_id: int32 [131072, 1], P(('slab', 'gy')), may hold values from 0 to 1023; in each aligned block of 1024 rows (0 to 1023, 1024 to 2047, ...) at most 2 rows name the same one
- transition: bfloat16 [1024, 256, 256], P(('slab', 'gy')), may hold values from -1 to 1
- forcing: float32 [1024, 3, 256], P(('slab', 'gy')), may hold values from -3 to 3
Outputs:
- final_field: float32 [3, 32, 256, 512], P(None, None, 'slab', 'gy')
- building_state: float32 [131072, 256], P(('slab', 'gy'))
Inputs may be any that keep to these rules, and one draw needn't show every extreme that they name: `cell_index`: building b's cell has x between s * 8 and s * 8 + 7, where s = (b // 1024) // 4; y is any. `archetype_id`: among the 1024 buildings of one device no archetype appears more than 2 times.
All inputs are finite; a program needn't handle non-finite values.
Results may differ from a plain program's by a relative error of at most 0.0023.
Values sent between devices are 32-bit elements; how exact they have to be, the bound alone decides.
No kernel may reach another device: no remote copies, remote signals or barrier semaphores. Data moves between devices by JAX's collectives and lax.ppermute only.
A program may use at most 64 MiB of HBM per device.

v0:
```python
import functools

import jax
import jax.numpy as jnp
import numpy as np
from jax import lax
from jax.experimental import pallas as pl
from jax.experimental.pallas import tpu as pltpu
from jax.sharding import PartitionSpec as P

COUPLINGS = 4
EVERY = 5
SUB = 6
NZ = 32
CX = 8
CY = 128
GROUPS = 4
ROWS = CY // GROUPS
STEPS = 4
HALO = 2 * STEPS
X0 = HALO + 2
XE = 2 * X0 + CX
R0 = 16
RE = 64
VMEM = pl.BlockSpec(memory_space=pltpu.VMEM)
SMEM = pl.BlockSpec(memory_space=pltpu.SMEM)


def depth_weights():
    z = np.arange(128) % NZ
    second = np.zeros((5, 128), np.float32)
    first = np.zeros((5, 128), np.float32)
    second[:] = np.array([-1, 16, -30, 16, -1], np.float32)[:, None]
    first[:] = np.array([1, -8, 0, 8, -1], np.float32)[:, None]
    for table in (second, first):
        for lane in range(128):
            for k in range(5):
                source = z[lane] + k - 2
                weight = table[k, lane]
                if source < 0:
                    table[k, lane] = 0.0
                    table[-source - z[lane] + 2, lane] += weight
                elif source >= NZ:
                    table[k, lane] = 0.0
    both = np.concatenate([second, first])
    return np.broadcast_to(both[:, None, :], (10, 8, 128)).copy()


def along_depth(value, weights):
    total = weights[2] * value
    for k, shift in ((0, 2), (1, 1), (3, 127), (4, 126)):
        total = total + weights[k] * pltpu.roll(value, shift, 1)
    return total


def advance(step, field, former, shear, bulk, part_x, part_y, part_z, weights_ref):
    row_a, tiles_a = R0 - HALO - 2 + 2 * step, -(-(ROWS + 2 * HALO + 4 - 4 * step) // 8)
    row_b, tiles_b = R0 - HALO + 2 * step, -(-(ROWS + 2 * HALO - 4 * step) // 8)

    def firsts(x, carry):
        first_z = [weights_ref[5 + k] for k in range(5)]
        for k in range(tiles_a):
            r = row_a + 8 * k
            at = lambda c, dx, dr: field[c, x + dx, pl.ds(r + dr, 8), :]
            along_z = along_depth(at(2, 0, 0), first_z)
            along_y = 8.0 * (at(1, 0, 1) - at(1, 0, -1)) - (at(1, 0, 2) - at(1, 0, -2))
            along_x = 8.0 * (at(0, 1, 0) - at(0, -1, 0)) - (at(0, 2, 0) - at(0, -2, 0))
            part_x[x, pl.ds(r, 8), :] = along_y + along_z
            part_y[x, pl.ds(r, 8), :] = along_x + along_z
            part_z[x, pl.ds(r, 8), :] = along_x + along_y
        return carry

    def update(x, carry):
        second_z = [weights_ref[k] for k in range(5)]
        first_z = [weights_ref[5 + k] for k in range(5)]
        for k in range(tiles_b):
            r = row_b + 8 * k
            rows = pl.ds(r, 8)
            s = shear[x, rows, :]
            b = bulk[x, rows, :]
            for c in range(3):
                at = lambda dx, dr: field[c, x + dx, pl.ds(r + dr, 8), :]
                centre = at(0, 0)
                d_x = 16.0 * (at(1, 0) + at(-1, 0)) - (at(2, 0) + at(-2, 0))
                d_y = 16.0 * (at(0, 1) + at(0, -1)) - (at(0, 2) + at(0, -2))
                d_z = along_depth(centre, second_z)
                if c == 0:
                    own = d_x - 30.0 * centre
                    mixed = 8.0 * (part_x[x + 1, rows, :] - part_x[x - 1, rows, :]) - (
                        part_x[x + 2, rows, :] - part_x[x - 2, rows, :]
                    )
                elif c == 1:
                    own = d_y - 30.0 * centre
                    mixed = 8.0 * (
                        part_y[x, pl.ds(r + 1, 8), :] - part_y[x, pl.ds(r - 1, 8), :]
                    ) - (part_y[x, pl.ds(r + 2, 8), :] - part_y[x, pl.ds(r - 2, 8), :])
                else:
                    own = d_z
                    mixed = along_depth(part_z[x, rows, :], first_z)
                laplacian = (d_x + d_y) + (d_z - 60.0 * centre)
                change = s * laplacian + b * (own + (1.0 / 12.0) * mixed)
                former[c, x, rows, :] = (2.0 * centre - former[c, x, rows, :]) + change
        return carry

    lax.fori_loop(2 * step, XE - 2 * step, firsts, 0)
    lax.fori_loop(2 * step + 2, XE - 2 * step - 2, update, 0)


def place_block(block, low, high, exists, x_from, targets):
    lane = lax.broadcasted_iota(jnp.int32, (8, 128), 1)
    here, from_low, from_high = exists

    def column(x, carry):
        for f, target in enumerate(targets):
            for k in range(ROWS // 8):
                value = jnp.where(here, block[f, x, pl.ds(8 * k, 8), :], 0.0)
                target[x_from + x, pl.ds(R0 + 8 * k, 8), :] = value
            last = jnp.where(here, block[f, x, pl.ds(ROWS - 8, 8), :], 0.0)
            head = jnp.where(here, block[f, x, pl.ds(0, 8), :], 0.0)
            below = jnp.where(from_low, low[f, x, :, :], 0.0)
            above = jnp.where(from_high, high[f, x, :, :], 0.0)
            target[x_from + x, pl.ds(R0 - 8, 8), :] = pltpu.roll(
                jnp.where(lane >= 96, below, last), 32, 1
            )
            target[x_from + x, pl.ds(R0 + ROWS, 8), :] = pltpu.roll(
                jnp.where(lane < 32, above, head), 96, 1
            )
        return carry

    lax.fori_loop(0, CX, column, 0)


def grid_kernel(first, snap_step, edge, weights_ref, *refs):
    blocks = [refs[3 * i : 3 * i + 3] for i in range(3)]
    refs = refs[9:]
    if first:
        out, low_out, high_out, shear, bulk = refs[:5]
        refs = refs[5:]
    else:
        shear, bulk, out, low_out, high_out = refs[:5]
        refs = refs[5:]
    snap = None
    if snap_step is not None:
        snap = refs[0]
        refs = refs[1:]
    fields = refs[:2]
    parts = refs[2:5]

    low_here, high_here = edge[2] == 1, edge[3] == 1
    for i, (block, low, high) in enumerate(blocks):
        here = (None, edge[0] == 1, edge[1] == 1)[i]
        x_from = (X0, X0 - CX, X0 + CX)[i]
        targets = [fields[f // 3].at[f % 3] for f in range(6)]
        if first:
            targets = targets + [shear, bulk]
        if here is None:
            exists = (low_here | high_here | True, low_here, high_here)
        else:
            exists = (
                here,
                jnp.logical_and(here, low_here),
                jnp.logical_and(here, high_here),
            )
        place_block(block, low, high, exists, x_from, targets)

    now, before = fields
    for step in range(1, STEPS + 1):
        advance(step, now, before, shear, bulk, *parts, weights_ref)
        now, before = before, now
        if step == snap_step:
            snap[...] = now[:, pl.ds(X0, CX), pl.ds(R0, ROWS), :]
    for f, source in ((0, now), (3, before)):
        out[pl.ds(f, 3)] = source[:, pl.ds(X0, CX), pl.ds(R0, ROWS), :]
        low_out[pl.ds(f, 3)] = source[:, pl.ds(X0, CX), pl.ds(R0, 8), :]
        high_out[pl.ds(f, 3)] = source[:, pl.ds(X0, CX), pl.ds(R0 + ROWS - 8, 8), :]


def run_grid(first, snap_step, edge, weights, arrays, coefs):
    shape = lambda *s: jax.ShapeDtypeStruct(s, jnp.float32)
    outs = [shape(6, CX, ROWS, 128), shape(6, CX, 8, 128), shape(6, CX, 8, 128)]
    operands = [edge, weights, *arrays]
    if first:
        outs += [shape(XE, RE, 128)] * 2
    else:
        operands += list(coefs)
    if snap_step is not None:
        outs.append(shape(3, CX, ROWS, 128))
    return pl.pallas_call(
        functools.partial(grid_kernel, first, snap_step),
        out_shape=outs,
        in_specs=[SMEM] + [VMEM] * (len(operands) - 1),
        out_specs=[VMEM] * len(outs),
        scratch_shapes=[pltpu.VMEM((3, XE, RE, 128), jnp.float32)] * 2
        + [pltpu.VMEM((XE, RE, 128), jnp.float32)] * 3,
        compiler_params=pltpu.CompilerParams(vmem_limit_bytes=40 << 20),
        cost_estimate=pl.CostEstimate(
            flops=40_000_000, bytes_accessed=8 << 20, transcendentals=0
        ),
        name="grid_steps",
    )(*operands)


def response_kernel(transition, forcing, out, state, total):
    arch = transition.shape[0]
    state[...] = jnp.zeros_like(state)
    out[...] = jnp.zeros_like(out)
    for a in range(arch):
        state[a, 0:3, :] = forcing[a]

    def one(j, carry):
        for a in range(arch):
            now = state[a]
            total[a] = total[a] + now
            high = now.astype(jnp.bfloat16)
            low = (now - high.astype(jnp.float32)).astype(jnp.bfloat16)
            product = lax.dot_general(
                jnp.concatenate([high, low], axis=0),
                transition[a],
                (((1,), (1,)), ((), ())),
                preferred_element_type=jnp.float32,
            )
            state[a] = product[0:8] + product[8:16]
        return carry

    for group in range(COUPLINGS):
        moment = COUPLINGS - 1 - group
        total[...] = jnp.zeros_like(total)
        lax.fori_loop(0, SUB, one, 0)
        for a in range(arch):
            for c in range(3):
                for h in range(2):
                    row = 2 * c + h
                    out[a, moment, row : row + 1, :] = total[
                        a, c : c + 1, 128 * h : 128 * h + 128
                    ]
            if group < COUPLINGS - 1:
                scale = jnp.maximum(jnp.max(jnp.abs(state[a]), keepdims=True), 1.0)
                state[a] = state[a] / scale
                out[a, moment, 6:7, :] = jnp.broadcast_to(scale, (1, 128))


def responses(transition, forcing):
    arch, width = transition.shape[0], transition.shape[1]
    return pl.pallas_call(
        response_kernel,
        out_shape=jax.ShapeDtypeStruct((arch, COUPLINGS, 8, 128), jnp.float32),
        in_specs=[VMEM, VMEM],
        out_specs=VMEM,
        scratch_shapes=[pltpu.VMEM((arch, 8, width), jnp.float32)] * 2,
        compiler_params=pltpu.CompilerParams(vmem_limit_bytes=24 << 20),
        cost_estimate=pl.CostEstimate(
            flops=20_000_000, bytes_accessed=2 << 20, transcendentals=0
        ),
        name="responses",
    )(transition, forcing)


def building_kernel(kinds, place, across, surface, table, out, ground):
    count = out.shape[0]
    cells = surface.shape[0] * CY
    picks = (lax.broadcasted_iota(jnp.int32, (cells, count), 0) == place[...]).astype(jnp.bfloat16)
    values = jnp.concatenate([surface[j] for j in range(surface.shape[0])], axis=1)
    high = values.astype(jnp.bfloat16)
    rest = values - high.astype(jnp.float32)
    low = rest.astype(jnp.bfloat16)
    least = (rest - low.astype(jnp.float32)).astype(jnp.bfloat16)
    picked = jnp.dot(
        jnp.concatenate([high, low, least], axis=0), picks, preferred_element_type=jnp.float32
    )
    n = values.shape[0]
    picked = picked[0:n] + picked[n : 2 * n] + picked[2 * n : 3 * n]
    here = lax.broadcasted_iota(jnp.int32, (CX, count), 0) == across[...]
    row = lax.broadcasted_iota(jnp.int32, (8, count), 0)
    for m in range(COUPLINGS):
        rows = []
        for c in range(3):
            k = 3 * m + c
            value = jnp.where(here, picked[CX * k : CX * k + CX], 0.0)
            rows.append(jnp.sum(value, axis=0, keepdims=True))
        ground[m] = jnp.where(
            row < 2, rows[0], jnp.where(row < 4, rows[1], jnp.where(row < 6, rows[2], 0.0))
        )

    def tile(t, carry):
        base = pl.multiple_of(t * 128, 128)
        motion = [ground[m, :, pl.ds(base, 128)] for m in range(COUPLINGS)]
        slot = lax.broadcasted_iota(jnp.int32, (8, 128), 0)
        for eight in range(16):
            halves = [jnp.zeros((8, 128), jnp.float32)] * 2
            for k in range(8):
                i = 8 * eight + k
                kind = kinds[base + i]
                total = None
                for m in range(COUPLINGS):
                    term = table[kind, m] * jnp.broadcast_to(motion[m][:, i : i + 1], (8, 128))
                    if total is None:
                        total = term
                    else:
                        scale = jnp.broadcast_to(table[kind, m, 6:7, :], (8, 128))
                        total = total * scale + term
                total = total + pltpu.roll(total, 4, 0)
                total = total + pltpu.roll(total, 2, 0)
                other = pltpu.roll(total, 1, 0)
                pair = (total, other) if k % 2 == 0 else (other, total)
                halves = [jnp.where(slot == k, new, old) for new, old in zip(pair, halves)]
            rows = pl.ds(base + 8 * eight, 8)
            out[rows, 0:128] = halves[0]
            out[rows, 128:256] = halves[1]
        return carry

    lax.fori_loop(0, count // 128, tile, 0)


def building_states(kinds, place, across, surface, table, width):
    count = kinds.shape[0]
    return pl.pallas_call(
        building_kernel,
        out_shape=jax.ShapeDtypeStruct((count, width), jnp.float32),
        in_specs=[SMEM] + [VMEM] * 4,
        out_specs=VMEM,
        scratch_shapes=[pltpu.VMEM((COUPLINGS, 8, count), jnp.float32)],
        compiler_params=pltpu.CompilerParams(vmem_limit_bytes=50 << 20),
        cost_estimate=pl.CostEstimate(
            flops=20_000_000, bytes_accessed=18 << 20, transcendentals=0
        ),
        name="buildings",
    )(kinds, place[None, :], across[None, :], surface, table)


def ring(value, axis, shift):
    count = lax.axis_size(axis)
    return lax.ppermute(value, axis, [(i, (i + shift) % count) for i in range(count)])


def exchange(own, top, bottom):
    low, high = ring(bottom, "gy", 1), ring(top, "gy", -1)
    arrays = [own, low, high]
    for shift in (1, -1):
        arrays += [ring(own, "slab", shift)]
        arrays += [ring(low, "slab", shift), ring(high, "slab", shift)]
    return arrays


def per_device(
    displacement, previous, shear_coef, bulk_coef, cell_index, archetype_id, transition, forcing
):
    width = transition.shape[1]
    slab, gy = lax.axis_index("slab"), lax.axis_index("gy")
    slabs, strips = lax.axis_size("slab"), lax.axis_size("gy")
    edge = jnp.stack([slab > 0, slab < slabs - 1, gy > 0, gy < strips - 1]).astype(jnp.int32)
    weights = jnp.asarray(depth_weights())

    stacked = jnp.concatenate(
        [displacement, previous, shear_coef[None] / 12.0, bulk_coef[None] / 12.0]
    )
    own = stacked.reshape(8, NZ, CX, GROUPS, ROWS).transpose(0, 2, 4, 3, 1)
    own = own.reshape(8, CX, ROWS, 128)
    arrays = exchange(own, own[:, :, :8], own[:, :, ROWS - 8 :])

    table = lax.all_gather(responses(transition, forcing), ("slab", "gy"), axis=0, tiled=True)

    snaps = []
    coefs = None
    blocks = COUPLINGS * EVERY // STEPS
    for block in range(blocks):
        snap_step = next(
            (s for s in range(1, STEPS + 1) if (block * STEPS + s) % EVERY == 0), None
        )
        result = run_grid(block == 0, snap_step, edge, weights, arrays, coefs)
        own, top, bottom = result[:3]
        if block == 0:
            coefs = result[3:5]
        if snap_step is not None:
            ground = result[-1][..., ::NZ]
            snaps.append(ground.transpose(0, 1, 3, 2).reshape(3 * CX, CY))
        if block < blocks - 1:
            arrays = exchange(own, top, bottom)
    final = own[:3].reshape(3, CX, ROWS, GROUPS, NZ).transpose(0, 4, 1, 3, 2)
    final = final.reshape(3, NZ, CX, CY)

    mine = jnp.concatenate(snaps)
    surface = jnp.stack([mine] + [ring(mine, "gy", shift) for shift in range(1, strips)])
    columns = strips * CY
    along_y = cell_index % columns
    across = cell_index // columns - slab * CX
    place = (gy - along_y // CY) % strips * CY + along_y % CY
    states = building_states(archetype_id[:, 0], place, across, surface, table, width)
    return (final, states)


def solution(mesh):
    in_specs = (
        P(None, None, "slab", "gy"),
        P(None, None, "slab", "gy"),
        P(None, "slab", "gy"),
        P(None, "slab", "gy"),
        P(("slab", "gy")),
        P(("slab", "gy"), None),
        P(("slab", "gy"), None, None),
        P(("slab", "gy"), None, None),
    )
    out_specs = (P(None, None, "slab", "gy"), P(("slab", "gy"), None))
    return jax.shard_map(
        per_device, mesh=mesh, in_specs=in_specs, out_specs=out_specs, check_vma=False
    )
```

profile of v0, /device:TPU:16, one launch (start us, length us, event | category | flops | bytes accessed | tf_op | source)
XLA Modules:
  0.0 317.7 jit_solution(8052726025573741510)
XLA Ops:
  8.0 1.2 copy-done.2
  9.2 10.4 %responses.1 = f32[8,4,8,128]{3,2,1,0:T(8,128)} custom-call(bf16[8,256,256]{2,1,0:T(8,128)(2,1)S(1)} %copy-done.2, f32[8,3,256]{2,1,0:T(4,128)S(1)} %copy.30.forcing), custom_call_target="tpu_custom_call" | custom-call | flops 20000000 | bytes 2097152 | tf_op jit(solution)/shard_map/responses/pallas_call | solution.py:244
  19.6 0.9 broadcast_multiply_fusion
  20.8 1.3 copy.24
  22.1 0.9 broadcast_multiply_fusion.1
  23.3 1.3 copy.23
  26.2 2.9 concatenate.15
  29.0 1.9 copy.21
  31.0 3.7 %maximum_bitcast_fusion = f32[8,8,32,4,32]{4,3,2,1,0:T(4,128)} fusion(f32[1,32,8,4,32]{1,3,4,2,0:T(4,128)} %copy.24, f32[1,32,8,4,32]{1,3,4,2,0:T(4,128)} %copy.23, f32[3,32,8,4,32]{1,3,4,2,0:T(4,128)S(1)} %copy.22, f32[3,32,8,4,32]{1,3,4,2,0:T(4,128)S(1)} %copy.21), kind=kLoop, calls=%fused_computation | loop fusion | flops 786432 | bytes 2097152 | tf_op jit(solution)/shard_map/transpose | solution.py:356
  34.6 3.7 %reshape.34.refs_0_ = f32[8,8,32,128]{3,2,1,0:T(8,128)S(1)} reshape(f32[8,8,32,4,32]{4,3,2,1,0:T(4,128)} %maximum_bitcast_fusion) | data formatting | bytes 2097152 | tf_op jit(solution)/shard_map/reshape | solution.py:357
  38.5 5.8 %collective-permute-start.5 = (f32[8,8,32,128]{3,2,1,0:T(8,128)S(1)}, f32[8,8,32,128]{3,2,1,0:T(8,128)}, u32[]{:S(2)}, u32[]{:S(2)}) collective-permute-start(f32[8,8,32,128]{3,2,1,0:T(8,128)S(1)} %reshape.34.refs_0_), channel_id=1, source_target_pairs={{0,124},{4,0},{8,4},{12,8},{16,12},{20,16},{24,20},{28,24},{32,28}... | collective-permute-start | bytes 3145736 | tf_op jit(solution)/shard_map/ppermute | solution.py:332
  44.3 1.3 collective-permute-start
  46.4 4.3 %collective-permute-done.refs_1_ = f32[8,8,8,128]{3,2,1,0:T(8,128)S(1)} collective-permute-done((f32[8,8,8,128]{3,2,1,0:T(8,128)S(1)}, f32[8,8,8,128]{3,2,1,0:T(8,128)S(1)}, u32[]{:S(2)}, u32[]{:S(2)}) %collective-permute-start) | collective-permute-done | bytes 262176 | tf_op jit(solution)/shard_map/ppermute | solution.py:332
  50.7 5.1 %collective-permute-start.6 = (f32[8,8,8,128]{3,2,1,0:T(8,128)S(1)}, f32[8,8,8,128]{3,2,1,0:T(8,128)S(1)}, u32[]{:S(2)}, u32[]{:S(2)}) collective-permute-start(f32[8,8,8,128]{3,2,1,0:T(8,128)S(1)} %collective-permute-done.refs_1_), channel_id=1, source_target_pairs={{0,124},{4,0},{8,4},{12,8},{16,12},{20,16},{24,20},{28,24},{32,28}... | collective-permute-start | bytes 786440 | tf_op jit(solution)/shard_map/ppermute | solution.py:332
  55.8 6.1 %collective-permute-done.3.refs_4_ = f32[8,8,8,128]{3,2,1,0:T(8,128)S(1)} collective-permute-done((f32[8,8,8,128]{3,2,1,0:T(8,128)S(1)}, f32[8,8,8,128]{3,2,1,0:T(8,128)S(1)}, u32[]{:S(2)}, u32[]{:S(2)}) %collective-permute-start.3) | collective-permute-done | bytes 262176 | tf_op jit(solution)/shard_map/ppermute | solution.py:332
  62.7 3.8 %collective-permute-done.4.refs_5_ = f32[8,8,8,128]{3,2,1,0:T(8,128)S(1)} collective-permute-done((f32[8,8,8,128]{3,2,1,0:T(8,128)S(1)}, f32[8,8,8,128]{3,2,1,0:T(8,128)S(1)}, u32[]{:S(2)}, u32[]{:S(2)}) %collective-permute-start.4) | collective-permute-done | bytes 262176 | tf_op jit(solution)/shard_map/ppermute | solution.py:332
  68.7 1.0 copy-done
  69.7 1.2 copy-done.1
  70.9 0.9 copy-done.6
  71.9 0.9 copy-done.8
  72.8 0.9 copy-done.10
  73.8 0.9 copy-done.12
  74.7 19.6 %grid_steps.5 = (f32[6,8,32,128]{3,2,1,0:T(8,128)S(1)}, f32[6,8,8,128]{3,2,1,0:T(8,128)S(1)}, f32[6,8,8,128]{3,2,1,0:T(8,128)S(1)}, f32[28,64,128]{2,1,0:T(8,128)S(1)}, f32[28,64,128]{2,1,0:T(8,128)S(1)}) custom-call(s32[4]{0:T(128)S(1)} %add_convert_fusion.edge, f32[10,8,128]{2,1,0:T(8,128)S(1)} %copy-done.3, f32[8,8,32,128]{3,2,1,0:T(8,128)S(1)} %reshape.34.refs_0_, ...), custom_call_target="tpu_custom_call" | custom-call | flops 40000000 | bytes 8388608 | tf_op jit(solution)/shard_map/grid_steps/pallas_call | solution.py:188
  94.4 5.3 %collective-permute-start.13 = (f32[6,8,32,128]{3,2,1,0:T(8,128)S(1)}, f32[6,8,32,128]{3,2,1,0:T(8,128)S(1)}, u32[]{:S(2)}, u32[]{:S(2)}) collective-permute-start(f32[6,8,32,128]{3,2,1,0:T(8,128)S(1)} %get-tuple-element.21.refs_0_), channel_id=1, source_target_pairs={{0,124},{4,0},{8,4},{12,8},{16,12},{20,16},{24,20},{28,24},{32,28}... | collective-permute-start | bytes 2359304 | tf_op jit(solution)/shard_map/ppermute | solution.py:332
  99.7 1.3 collective-permute-start.8
  101.8 3.6 %collective-permute-done.8.refs_1_ = f32[6,8,8,128]{3,2,1,0:T(8,128)S(1)} collective-permute-done((f32[6,8,8,128]{3,2,1,0:T(8,128)S(1)}, f32[6,8,8,128]{3,2,1,0:T(8,128)S(1)}, u32[]{:S(2)}, u32[]{:S(2)}) %collective-permute-start.8) | collective-permute-done | bytes 196640 | tf_op jit(solution)/shard_map/ppermute | solution.py:332
  105.4 5.1 %collective-permute-start.14 = (f32[6,8,8,128]{3,2,1,0:T(8,128)S(1)}, f32[6,8,8,128]{3,2,1,0:T(8,128)S(1)}, u32[]{:S(2)}, u32[]{:S(2)}) collective-permute-start(f32[6,8,8,128]{3,2,1,0:T(8,128)S(1)} %collective-permute-done.8.refs_1_), channel_id=1, source_target_pairs={{0,124},{4,0},{8,4},{12,8},{16,12},{20,16},{24,20},{28,24},{32,28}... | collective-permute-start | bytes 589832 | tf_op jit(solution)/shard_map/ppermute | solution.py:332
  110.5 5.3 %collective-permute-done.11.refs_4_ = f32[6,8,8,128]{3,2,1,0:T(8,128)S(1)} collective-permute-done((f32[6,8,8,128]{3,2,1,0:T(8,128)S(1)}, f32[6,8,8,128]{3,2,1,0:T(8,128)S(1)}, u32[]{:S(2)}, u32[]{:S(2)}) %collective-permute-start.11) | collective-permute-done | bytes 196640 | tf_op jit(solution)/shard_map/ppermute | solution.py:332
  115.8 3.1 collective-permute-done.12.refs_5_
  119.0 19.0 %grid_steps.6 = (f32[6,8,32,128]{3,2,1,0:T(8,128)S(1)}, f32[6,8,8,128]{3,2,1,0:T(8,128)S(1)}, f32[6,8,8,128]{3,2,1,0:T(8,128)S(1)}, f32[3,8,32,128]{3,2,1,0:T(8,128)S(1)}) custom-call(s32[4]{0:T(128)S(1)} %add_convert_fusion.edge, f32[10,8,128]{2,1,0:T(8,128)S(1)} %copy-done.3, f32[6,8,32,128]{3,2,1,0:T(8,128)S(1)} %get-tuple-element.21.refs_0_, ...), custom_call_target="tpu_custom_call" | custom-call | flops 40000000 | bytes 8388608 | tf_op jit(solution)/shard_map/grid_steps/pallas_call | solution.py:188
  138.1 5.3 %collective-permute-start.21 = (f32[6,8,32,128]{3,2,1,0:T(8,128)S(1)}, f32[6,8,32,128]{3,2,1,0:T(8,128)S(1)}, u32[]{:S(2)}, u32[]{:S(2)}) collective-permute-start(f32[6,8,32,128]{3,2,1,0:T(8,128)S(1)} %get-tuple-element.26.refs_0_), channel_id=1, source_target_pairs={{0,124},{4,0},{8,4},{12,8},{16,12},{20,16},{24,20},{28,24},{32,28}... | collective-permute-start | bytes 2359304 | tf_op jit(solution)/shard_map/ppermute | solution.py:332
  143.4 1.4 collective-permute-start.16
  145.4 3.6 %collective-permute-done.16.refs_1_ = f32[6,8,8,128]{3,2,1,0:T(8,128)S(1)} collective-permute-done((f32[6,8,8,128]{3,2,1,0:T(8,128)S(1)}, f32[6,8,8,128]{3,2,1,0:T(8,128)S(1)}, u32[]{:S(2)}, u32[]{:S(2)}) %collective-permute-start.16) | collective-permute-done | bytes 196640 | tf_op jit(solution)/shard_map/ppermute | solution.py:332
  149.0 5.1 %collective-permute-start.22 = (f32[6,8,8,128]{3,2,1,0:T(8,128)S(1)}, f32[6,8,8,128]{3,2,1,0:T(8,128)S(1)}, u32[]{:S(2)}, u32[]{:S(2)}) collective-permute-start(f32[6,8,8,128]{3,2,1,0:T(8,128)S(1)} %collective-permute-done.16.refs_1_), channel_id=1, source_target_pairs={{0,124},{4,0},{8,4},{12,8},{16,12},{20,16},{24,20},{28,24},{32,28}... | collective-permute-start | bytes 589832 | tf_op jit(solution)/shard_map/ppermute | solution.py:332
  154.1 3.3 %collective-permute-done.19.refs_4_ = f32[6,8,8,128]{3,2,1,0:T(8,128)S(1)} collective-permute-done((f32[6,8,8,128]{3,2,1,0:T(8,128)S(1)}, f32[6,8,8,128]{3,2,1,0:T(8,128)S(1)}, u32[]{:S(2)}, u32[]{:S(2)}) %collective-permute-start.19) | collective-permute-done | bytes 196640 | tf_op jit(solution)/shard_map/ppermute | solution.py:332
  157.5 1.7 collective-permute-start.23
  159.2 3.3 %collective-permute-done.20.refs_5_ = f32[6,8,8,128]{3,2,1,0:T(8,128)S(1)} collective-permute-done((f32[6,8,8,128]{3,2,1,0:T(8,128)S(1)}, f32[6,8,8,128]{3,2,1,0:T(8,128)S(1)}, u32[]{:S(2)}, u32[]{:S(2)}) %collective-permute-start.20) | collective-permute-done | bytes 196640 | tf_op jit(solution)/shard_map/ppermute | solution.py:332
  162.5 19.0 %grid_steps.7 = (f32[6,8,32,128]{3,2,1,0:T(8,128)S(1)}, f32[6,8,8,128]{3,2,1,0:T(8,128)S(1)}, f32[6,8,8,128]{3,2,1,0:T(8,128)S(1)}, f32[3,8,32,128]{3,2,1,0:T(8,128)S(1)}) custom-call(s32[4]{0:T(128)S(1)} %add_convert_fusion.edge, f32[10,8,128]{2,1,0:T(8,128)S(1)} %copy-done.3, f32[6,8,32,128]{3,2,1,0:T(8,128)S(1)} %get-tuple-element.26.refs_0_, ...), custom_call_target="tpu_custom_call" | custom-call | flops 40000000 | bytes 8388608 | tf_op jit(solution)/shard_map/grid_steps/pallas_call | solution.py:188
  181.6 5.1 %collective-permute-start.29 = (f32[6,8,32,128]{3,2,1,0:T(8,128)S(1)}, f32[6,8,32,128]{3,2,1,0:T(8,128)S(1)}, u32[]{:S(2)}, u32[]{:S(2)}) collective-permute-start(f32[6,8,32,128]{3,2,1,0:T(8,128)S(1)} %get-tuple-element.29.refs_0_), channel_id=1, source_target_pairs={{0,124},{4,0},{8,4},{12,8},{16,12},{20,16},{24,20},{28,24},{32,28}... | collective-permute-start | bytes 2359304 | tf_op jit(solution)/shard_map/ppermute | solution.py:332
  186.8 2.6 collective-permute-start.24
  189.4 3.5 %collective-permute-done.24.refs_1_ = f32[6,8,8,128]{3,2,1,0:T(8,128)S(1)} collective-permute-done((f32[6,8,8,128]{3,2,1,0:T(8,128)S(1)}, f32[6,8,8,128]{3,2,1,0:T(8,128)S(1)}, u32[]{:S(2)}, u32[]{:S(2)}) %collective-permute-start.24) | collective-permute-done | bytes 196640 | tf_op jit(solution)/shard_map/ppermute | solution.py:332
  192.9 5.1 %collective-permute-start.30 = (f32[6,8,8,128]{3,2,1,0:T(8,128)S(1)}, f32[6,8,8,128]{3,2,1,0:T(8,128)S(1)}, u32[]{:S(2)}, u32[]{:S(2)}) collective-permute-start(f32[6,8,8,128]{3,2,1,0:T(8,128)S(1)} %collective-permute-done.24.refs_1_), channel_id=1, source_target_pairs={{0,124},{4,0},{8,4},{12,8},{16,12},{20,16},{24,20},{28,24},{32,28}... | collective-permute-start | bytes 589832 | tf_op jit(solution)/shard_map/ppermute | solution.py:332
  197.9 3.3 %collective-permute-done.27.refs_4_ = f32[6,8,8,128]{3,2,1,0:T(8,128)S(1)} collective-permute-done((f32[6,8,8,128]{3,2,1,0:T(8,128)S(1)}, f32[6,8,8,128]{3,2,1,0:T(8,128)S(1)}, u32[]{:S(2)}, u32[]{:S(2)}) %collective-permute-start.27) | collective-permute-done | bytes 196640 | tf_op jit(solution)/shard_map/ppermute | solution.py:332
  201.3 1.7 collective-permute-start.31
  203.0 3.3 %collective-permute-done.28.refs_5_ = f32[6,8,8,128]{3,2,1,0:T(8,128)S(1)} collective-permute-done((f32[6,8,8,128]{3,2,1,0:T(8,128)S(1)}, f32[6,8,8,128]{3,2,1,0:T(8,128)S(1)}, u32[]{:S(2)}, u32[]{:S(2)}) %collective-permute-start.28) | collective-permute-done | bytes 196640 | tf_op jit(solution)/shard_map/ppermute | solution.py:332
  206.4 19.6 %grid_steps.8 = (f32[6,8,32,128]{3,2,1,0:T(8,128)S(1)}, f32[6,8,8,128]{3,2,1,0:T(8,128)}, f32[6,8,8,128]{3,2,1,0:T(8,128)S(1)}, f32[3,8,32,128]{3,2,1,0:T(8,128)S(1)}) custom-call(s32[4]{0:T(128)S(1)} %add_convert_fusion.edge, f32[10,8,128]{2,1,0:T(8,128)S(1)} %copy-done.3, f32[6,8,32,128]{3,2,1,0:T(8,128)S(1)} %get-tuple-element.29.refs_0_, ...), custom_call_target="tpu_custom_call" | custom-call | flops 40000000 | bytes 8388608 | tf_op jit(solution)/shard_map/grid_steps/pallas_call | solution.py:188
  226.8 5.1 %collective-permute-start.37 = (f32[6,8,32,128]{3,2,1,0:T(8,128)S(1)}, f32[6,8,32,128]{3,2,1,0:T(8,128)}, u32[]{:S(2)}, u32[]{:S(2)}) collective-permute-start(f32[6,8,32,128]{3,2,1,0:T(8,128)S(1)} %get-tuple-element.32.refs_0_), channel_id=1, source_target_pairs={{0,124},{4,0},{8,4},{12,8},{16,12},{20,16},{24,20},{28,24},{32,28}... | collective-permute-start | bytes 2359304 | tf_op jit(solution)/shard_map/ppermute | solution.py:332
  231.8 3.4 %collective-permute-start.32 = (f32[6,8,8,128]{3,2,1,0:T(8,128)S(1)}, f32[6,8,8,128]{3,2,1,0:T(8,128)}, u32[]{:S(2)}, u32[]{:S(2)}) collective-permute-start(f32[6,8,8,128]{3,2,1,0:T(8,128)S(1)} %get-tuple-element.33), channel_id=1, source_target_pairs={{0,1},{1,2},{2,3},{3,0},{4,5},{5,6},{6,7},{7,4},{8,9},{9,10},{10,1... | collective-permute-start | bytes 589832 | tf_op jit(solution)/shard_map/ppermute | solution.py:332
  235.2 3.6 %collective-permute-done.32.refs_1_ = f32[6,8,8,128]{3,2,1,0:T(8,128)} collective-permute-done((f32[6,8,8,128]{3,2,1,0:T(8,128)S(1)}, f32[6,8,8,128]{3,2,1,0:T(8,128)}, u32[]{:S(2)}, u32[]{:S(2)}) %collective-permute-start.32) | collective-permute-done | bytes 196640 | tf_op jit(solution)/shard_map/ppermute | solution.py:332
  238.8 2.4 slice.24
  241.2 1.2 copy.26
  243.7 5.1 %collective-permute-start.38 = (f32[6,8,8,128]{3,2,1,0:T(8,128)}, f32[6,8,8,128]{3,2,1,0:T(8,128)S(1)}, u32[]{:S(2)}, u32[]{:S(2)}) collective-permute-start(f32[6,8,8,128]{3,2,1,0:T(8,128)} %collective-permute-done.32.refs_1_), channel_id=1, source_target_pairs={{0,124},{4,0},{8,4},{12,8},{16,12},{20,16},{24,20},{28,24},{32,28}... | collective-permute-start | bytes 589832 | tf_op jit(solution)/shard_map/ppermute | solution.py:332
  248.9 5.1 %collective-permute-start.39 = (f32[6,8,8,128]{3,2,1,0:T(8,128)}, f32[6,8,8,128]{3,2,1,0:T(8,128)S(1)}, u32[]{:S(2)}, u32[]{:S(2)}) collective-permute-start(f32[6,8,8,128]{3,2,1,0:T(8,128)} %collective-permute-done.33.refs_2_), channel_id=1, source_target_pairs={{0,124},{4,0},{8,4},{12,8},{16,12},{20,16},{24,20},{28,24},{32,28}... | collective-permute-start | bytes 589832 | tf_op jit(solution)/shard_map/ppermute | solution.py:332
  253.9 4.2 %slice.26 = f32[3,8,32,4]{3,2,1,0:T(8,128)} slice(f32[3,8,32,128]{3,2,1,0:T(8,128)} %copy-done.4), slice={[0:3:1], [0:8:1], [0:32:1], [0:128:32]} | slice | bytes 24576 | tf_op jit(solution)/shard_map/slice | solution.py:374
  258.1 1.2 copy.28
  260.1 0.9 copy-done.14
  261.1 20.8 %grid_steps.9 = (f32[6,8,32,128]{3,2,1,0:T(8,128)S(1)}, f32[6,8,8,128]{3,2,1,0:T(8,128)}, f32[6,8,8,128]{3,2,1,0:T(8,128)}, f32[3,8,32,128]{3,2,1,0:T(8,128)S(1)}) custom-call(s32[4]{0:T(128)S(1)} %add_convert_fusion.edge, f32[10,8,128]{2,1,0:T(8,128)S(1)} %copy-done.3, f32[6,8,32,128]{3,2,1,0:T(8,128)S(1)} %get-tuple-element.32.refs_0_, ...), custom_call_target="tpu_custom_call" | custom-call | flops 40000000 | bytes 8388608 | tf_op jit(solution)/shard_map/grid_steps/pallas_call | solution.py:188
  283.9 3.3 %collective-permute-start.42 = (f32[96,128]{1,0:T(8,128)S(1)}, f32[96,128]{1,0:T(8,128)S(1)}, u32[]{:S(2)}, u32[]{:S(2)}) collective-permute-start(f32[96,128]{1,0:T(8,128)S(1)} %constant_dynamic-update-slice_fusion), channel_id=1, source_target_pairs={{0,3},{1,0},{2,1},{3,2},{4,7},{5,4},{6,5},{7,6},{8,11},{9,8},{10,9... | collective-permute-start | bytes 147464 | tf_op jit(solution)/shard_map/ppermute | solution.py:332
  287.2 2.8 collective-permute-start.41
  290.0 2.5 collective-permute-start.40
  292.6 1.0 slice.23
  294.3 1.2 copy.25
  295.5 1.4 reshape.36
  297.0 13.9 %buildings.1 = f32[1024,256]{1,0:T(8,128)} custom-call(s32[1024]{0:T(1024)S(1)} %bitcast.26, s32[1,1024]{1,0:T(1,128)S(1)} %bitcast.25, s32[1,1024]{1,0:T(1,128)S(1)} %bitcast.24, f32[4,96,128]{2,1,0:T(8,128)S(1)} %pad_maximum_fusion.surface, f32[1024,4,8,128]{3,2,1,0:T(8,128)} %all-gather.2.cloned.1.call-done.table), custom_call_target="tpu_custom_call" | custom-call | flops 20000000 | bytes 18874368 | tf_op jit(solution)/shard_map/buildings/pallas_call | solution.py:316
  (107 shorter events, 14.1 us)
Async XLA Ops:
  7.2 289.9 %all-gather.2.cloned.1.call-start = ((), (), s32[]{:S(2)}) async-start(), calls=%async_computation | async-start | bytes 16908288 | tf_op jit(solution)/shard_map/all_gather | solution.py:360
  8.0 1.2 copy-start.2
  9.2 15.4 %copy-start.17 = (f32[3,32,8,128]{3,2,1,0:T(8,128)S(1)}, f32[3,32,8,128]{3,2,1,0:T(8,128)}, u32[]{:S(2)}) copy-start(f32[3,32,8,128]{3,2,1,0:T(8,128)} %param.10) | copy-start | bytes 1179652
  34.6 35.1 %copy-start.3 = (f32[10,8,128]{2,1,0:T(8,128)S(1)}, f32[10,8,128]{2,1,0:T(8,128)}, u32[]{:S(2)}) copy-start(f32[10,8,128]{2,1,0:T(8,128)} %constant.81.clone.weights_ref) | copy-start | bytes 122884
  38.4 30.4 %collective-permute-start.2 = (f32[8,8,32,128]{3,2,1,0:T(8,128)S(1)}, f32[8,8,32,128]{3,2,1,0:T(8,128)S(1)}, u32[]{:S(2)}, u32[]{:S(2)}) collective-permute-start(f32[8,8,32,128]{3,2,1,0:T(8,128)S(1)} %reshape.34.refs_0_), channel_id=1, source_target_pairs={{0,4},{4,8},{8,12},{12,16},{16,20},{20,24},{24,28},{28,32},{32,36}... | collective-permute-start | bytes 3145736 | tf_op jit(solution)/shard_map/ppermute | solution.py:332
  38.5 31.3 %collective-permute-start.5 = (f32[8,8,32,128]{3,2,1,0:T(8,128)S(1)}, f32[8,8,32,128]{3,2,1,0:T(8,128)}, u32[]{:S(2)}, u32[]{:S(2)}) collective-permute-start(f32[8,8,32,128]{3,2,1,0:T(8,128)S(1)} %reshape.34.refs_0_), channel_id=1, source_target_pairs={{0,124},{4,0},{8,4},{12,8},{16,12},{20,16},{24,20},{28,24},{32,28}... | collective-permute-start | bytes 3145736 | tf_op jit(solution)/shard_map/ppermute | solution.py:332
  44.3 6.4 %collective-permute-start = (f32[8,8,8,128]{3,2,1,0:T(8,128)S(1)}, f32[8,8,8,128]{3,2,1,0:T(8,128)S(1)}, u32[]{:S(2)}, u32[]{:S(2)}) collective-permute-start(f32[8,8,8,128]{3,2,1,0:T(8,128)S(1)} %get-tuple-element.41), channel_id=1, source_target_pairs={{0,1},{1,2},{2,3},{3,0},{4,5},{5,6},{6,7},{7,4},{8,9},{9,10},{10,1... | collective-permute-start | bytes 786440 | tf_op jit(solution)/shard_map/ppermute | solution.py:332
  45.6 10.2 %collective-permute-start.1 = (f32[8,8,8,128]{3,2,1,0:T(8,128)S(1)}, f32[8,8,8,128]{3,2,1,0:T(8,128)S(1)}, u32[]{:S(2)}, u32[]{:S(2)}) collective-permute-start(f32[8,8,8,128]{3,2,1,0:T(8,128)S(1)} %get-tuple-element.40), channel_id=1, source_target_pairs={{0,3},{1,0},{2,1},{3,2},{4,7},{5,4},{6,5},{7,6},{8,11},{9,8},{10,9... | collective-permute-start | bytes 786440 | tf_op jit(solution)/shard_map/ppermute | solution.py:332
  50.7 11.2 %collective-permute-start.3 = (f32[8,8,8,128]{3,2,1,0:T(8,128)S(1)}, f32[8,8,8,128]{3,2,1,0:T(8,128)S(1)}, u32[]{:S(2)}, u32[]{:S(2)}) collective-permute-start(f32[8,8,8,128]{3,2,1,0:T(8,128)S(1)} %collective-permute-done.refs_1_), channel_id=1, source_target_pairs={{0,4},{4,8},{8,12},{12,16},{16,20},{20,24},{24,28},{28,32},{32,36}... | collective-permute-start | bytes 786440 | tf_op jit(solution)/shard_map/ppermute | solution.py:332
  50.7 16.5 %collective-permute-start.6 = (f32[8,8,8,128]{3,2,1,0:T(8,128)S(1)}, f32[8,8,8,128]{3,2,1,0:T(8,128)S(1)}, u32[]{:S(2)}, u32[]{:S(2)}) collective-permute-start(f32[8,8,8,128]{3,2,1,0:T(8,128)S(1)} %collective-permute-done.refs_1_), channel_id=1, source_target_pairs={{0,124},{4,0},{8,4},{12,8},{16,12},{20,16},{24,20},{28,24},{32,28}... | collective-permute-start | bytes 786440 | tf_op jit(solution)/shard_map/ppermute | solution.py:332
  55.8 10.7 %collective-permute-start.4 = (f32[8,8,8,128]{3,2,1,0:T(8,128)S(1)}, f32[8,8,8,128]{3,2,1,0:T(8,128)S(1)}, u32[]{:S(2)}, u32[]{:S(2)}) collective-permute-start(f32[8,8,8,128]{3,2,1,0:T(8,128)S(1)} %collective-permute-done.1.refs_2_), channel_id=1, source_target_pairs={{0,4},{4,8},{8,12},{12,16},{16,20},{20,24},{24,28},{28,32},{32,36}... | collective-permute-start | bytes 786440 | tf_op jit(solution)/shard_map/ppermute | solution.py:332
  61.9 0.7 copy-start.5
  62.6 5.4 %collective-permute-start.7 = (f32[8,8,8,128]{3,2,1,0:T(8,128)S(1)}, f32[8,8,8,128]{3,2,1,0:T(8,128)S(1)}, u32[]{:S(2)}, u32[]{:S(2)}) collective-permute-start(f32[8,8,8,128]{3,2,1,0:T(8,128)S(1)} %collective-permute-done.1.refs_2_), channel_id=1, source_target_pairs={{0,124},{4,0},{8,4},{12,8},{16,12},{20,16},{24,20},{28,24},{32,28}... | collective-permute-start | bytes 786440 | tf_op jit(solution)/shard_map/ppermute | solution.py:332
  66.5 0.7 copy-start.9
  67.2 0.7 copy-start.7
  68.0 0.7 copy-start.11
  68.7 1.0 copy-start
  69.7 1.2 copy-start.1
  70.9 0.9 copy-start.6
  71.9 0.9 copy-start.8
  72.8 0.9 copy-start.10
  73.8 0.9 copy-start.12
  94.3 24.6 %collective-permute-start.10 = (f32[6,8,32,128]{3,2,1,0:T(8,128)S(1)}, f32[6,8,32,128]{3,2,1,0:T(8,128)S(1)}, u32[]{:S(2)}, u32[]{:S(2)}) collective-permute-start(f32[6,8,32,128]{3,2,1,0:T(8,128)S(1)} %get-tuple-element.21.refs_0_), channel_id=1, source_target_pairs={{0,4},{4,8},{8,12},{12,16},{16,20},{20,24},{24,28},{28,32},{32,36}... | collective-permute-start | bytes 2359304 | tf_op jit(solution)/shard_map/ppermute | solution.py:332
  94.4 24.6 %collective-permute-start.13 = (f32[6,8,32,128]{3,2,1,0:T(8,128)S(1)}, f32[6,8,32,128]{3,2,1,0:T(8,128)S(1)}, u32[]{:S(2)}, u32[]{:S(2)}) collective-permute-start(f32[6,8,32,128]{3,2,1,0:T(8,128)S(1)} %get-tuple-element.21.refs_0_), channel_id=1, source_target_pairs={{0,124},{4,0},{8,4},{12,8},{16,12},{20,16},{24,20},{28,24},{32,28}... | collective-permute-start | bytes 2359304 | tf_op jit(solution)/shard_map/ppermute | solution.py:332
  99.7 5.7 %collective-permute-start.8 = (f32[6,8,8,128]{3,2,1,0:T(8,128)S(1)}, f32[6,8,8,128]{3,2,1,0:T(8,128)S(1)}, u32[]{:S(2)}, u32[]{:S(2)}) collective-permute-start(f32[6,8,8,128]{3,2,1,0:T(8,128)S(1)} %get-tuple-element.22), channel_id=1, source_target_pairs={{0,1},{1,2},{2,3},{3,0},{4,5},{5,6},{6,7},{7,4},{8,9},{9,10},{10,1... | collective-permute-start | bytes 589832 | tf_op jit(solution)/shard_map/ppermute | solution.py:332
  101.1 9.4 %collective-permute-start.9 = (f32[6,8,8,128]{3,2,1,0:T(8,128)S(1)}, f32[6,8,8,128]{3,2,1,0:T(8,128)S(1)}, u32[]{:S(2)}, u32[]{:S(2)}) collective-permute-start(f32[6,8,8,128]{3,2,1,0:T(8,128)S(1)} %get-tuple-element.23), channel_id=1, source_target_pairs={{0,3},{1,0},{2,1},{3,2},{4,7},{5,4},{6,5},{7,6},{8,11},{9,8},{10,9... | collective-permute-start | bytes 589832 | tf_op jit(solution)/shard_map/ppermute | solution.py:332
  105.4 10.4 %collective-permute-start.11 = (f32[6,8,8,128]{3,2,1,0:T(8,128)S(1)}, f32[6,8,8,128]{3,2,1,0:T(8,128)S(1)}, u32[]{:S(2)}, u32[]{:S(2)}) collective-permute-start(f32[6,8,8,128]{3,2,1,0:T(8,128)S(1)} %collective-permute-done.8.refs_1_), channel_id=1, source_target_pairs={{0,4},{4,8},{8,12},{12,16},{16,20},{20,24},{24,28},{28,32},{32,36}... | collective-permute-start | bytes 589832 | tf_op jit(solution)/shard_map/ppermute | solution.py:332
  105.4 13.5 %collective-permute-start.14 = (f32[6,8,8,128]{3,2,1,0:T(8,128)S(1)}, f32[6,8,8,128]{3,2,1,0:T(8,128)S(1)}, u32[]{:S(2)}, u32[]{:S(2)}) collective-permute-start(f32[6,8,8,128]{3,2,1,0:T(8,128)S(1)} %collective-permute-done.8.refs_1_), channel_id=1, source_target_pairs={{0,124},{4,0},{8,4},{12,8},{16,12},{20,16},{24,20},{28,24},{32,28}... | collective-permute-start | bytes 589832 | tf_op jit(solution)/shard_map/ppermute | solution.py:332
  110.5 8.4 %collective-permute-start.12 = (f32[6,8,8,128]{3,2,1,0:T(8,128)S(1)}, f32[6,8,8,128]{3,2,1,0:T(8,128)S(1)}, u32[]{:S(2)}, u32[]{:S(2)}) collective-permute-start(f32[6,8,8,128]{3,2,1,0:T(8,128)S(1)} %collective-permute-done.9.refs_2_), channel_id=1, source_target_pairs={{0,4},{4,8},{8,12},{12,16},{16,20},{20,24},{24,28},{28,32},{32,36}... | collective-permute-start | bytes 589832 | tf_op jit(solution)/shard_map/ppermute | solution.py:332
  115.8 3.2 %collective-permute-start.15 = (f32[6,8,8,128]{3,2,1,0:T(8,128)S(1)}, f32[6,8,8,128]{3,2,1,0:T(8,128)S(1)}, u32[]{:S(2)}, u32[]{:S(2)}) collective-permute-start(f32[6,8,8,128]{3,2,1,0:T(8,128)S(1)} %collective-permute-done.9.refs_2_), channel_id=1, source_target_pairs={{0,124},{4,0},{8,4},{12,8},{16,12},{20,16},{24,20},{28,24},{32,28}... | collective-permute-start | bytes 589832 | tf_op jit(solution)/shard_map/ppermute | solution.py:332
  138.0 24.5 %collective-permute-start.18 = (f32[6,8,32,128]{3,2,1,0:T(8,128)S(1)}, f32[6,8,32,128]{3,2,1,0:T(8,128)S(1)}, u32[]{:S(2)}, u32[]{:S(2)}) collective-permute-start(f32[6,8,32,128]{3,2,1,0:T(8,128)S(1)} %get-tuple-element.26.refs_0_), channel_id=1, source_target_pairs={{0,4},{4,8},{8,12},{12,16},{16,20},{20,24},{24,28},{28,32},{32,36}... | collective-permute-start | bytes 2359304 | tf_op jit(solution)/shard_map/ppermute | solution.py:332
  138.1 24.5 %collective-permute-start.21 = (f32[6,8,32,128]{3,2,1,0:T(8,128)S(1)}, f32[6,8,32,128]{3,2,1,0:T(8,128)S(1)}, u32[]{:S(2)}, u32[]{:S(2)}) collective-permute-start(f32[6,8,32,128]{3,2,1,0:T(8,128)S(1)} %get-tuple-element.26.refs_0_), channel_id=1, source_target_pairs={{0,124},{4,0},{8,4},{12,8},{16,12},{20,16},{24,20},{28,24},{32,28}... | collective-permute-start | bytes 2359304 | tf_op jit(solution)/shard_map/ppermute | solution.py:332
  143.4 5.7 %collective-permute-start.16 = (f32[6,8,8,128]{3,2,1,0:T(8,128)S(1)}, f32[6,8,8,128]{3,2,1,0:T(8,128)S(1)}, u32[]{:S(2)}, u32[]{:S(2)}) collective-permute-start(f32[6,8,8,128]{3,2,1,0:T(8,128)S(1)} %get-tuple-element.27), channel_id=1, source_target_pairs={{0,1},{1,2},{2,3},{3,0},{4,5},{5,6},{6,7},{7,4},{8,9},{9,10},{10,1... | collective-permute-start | bytes 589832 | tf_op jit(solution)/shard_map/ppermute | solution.py:332
  144.8 9.3 %collective-permute-start.17 = (f32[6,8,8,128]{3,2,1,0:T(8,128)S(1)}, f32[6,8,8,128]{3,2,1,0:T(8,128)S(1)}, u32[]{:S(2)}, u32[]{:S(2)}) collective-permute-start(f32[6,8,8,128]{3,2,1,0:T(8,128)S(1)} %get-tuple-element.28), channel_id=1, source_target_pairs={{0,3},{1,0},{2,1},{3,2},{4,7},{5,4},{6,5},{7,6},{8,11},{9,8},{10,9... | collective-permute-start | bytes 589832 | tf_op jit(solution)/shard_map/ppermute | solution.py:332
  149.0 8.4 %collective-permute-start.19 = (f32[6,8,8,128]{3,2,1,0:T(8,128)S(1)}, f32[6,8,8,128]{3,2,1,0:T(8,128)S(1)}, u32[]{:S(2)}, u32[]{:S(2)}) collective-permute-start(f32[6,8,8,128]{3,2,1,0:T(8,128)S(1)} %collective-permute-done.16.refs_1_), channel_id=1, source_target_pairs={{0,4},{4,8},{8,12},{12,16},{16,20},{20,24},{24,28},{28,32},{32,36}... | collective-permute-start | bytes 589832 | tf_op jit(solution)/shard_map/ppermute | solution.py:332
  149.0 13.5 %collective-permute-start.22 = (f32[6,8,8,128]{3,2,1,0:T(8,128)S(1)}, f32[6,8,8,128]{3,2,1,0:T(8,128)S(1)}, u32[]{:S(2)}, u32[]{:S(2)}) collective-permute-start(f32[6,8,8,128]{3,2,1,0:T(8,128)S(1)} %collective-permute-done.16.refs_1_), channel_id=1, source_target_pairs={{0,124},{4,0},{8,4},{12,8},{16,12},{20,16},{24,20},{28,24},{32,28}... | collective-permute-start | bytes 589832 | tf_op jit(solution)/shard_map/ppermute | solution.py:332
  154.1 8.4 %collective-permute-start.20 = (f32[6,8,8,128]{3,2,1,0:T(8,128)S(1)}, f32[6,8,8,128]{3,2,1,0:T(8,128)S(1)}, u32[]{:S(2)}, u32[]{:S(2)}) collective-permute-start(f32[6,8,8,128]{3,2,1,0:T(8,128)S(1)} %collective-permute-done.17.refs_2_), channel_id=1, source_target_pairs={{0,4},{4,8},{8,12},{12,16},{16,20},{20,24},{24,28},{28,32},{32,36}... | collective-permute-start | bytes 589832 | tf_op jit(solution)/shard_map/ppermute | solution.py:332
  157.5 5.1 %collective-permute-start.23 = (f32[6,8,8,128]{3,2,1,0:T(8,128)S(1)}, f32[6,8,8,128]{3,2,1,0:T(8,128)S(1)}, u32[]{:S(2)}, u32[]{:S(2)}) collective-permute-start(f32[6,8,8,128]{3,2,1,0:T(8,128)S(1)} %collective-permute-done.17.refs_2_), channel_id=1, source_target_pairs={{0,124},{4,0},{8,4},{12,8},{16,12},{20,16},{24,20},{28,24},{32,28}... | collective-permute-start | bytes 589832 | tf_op jit(solution)/shard_map/ppermute | solution.py:332
  181.6 24.8 %collective-permute-start.26 = (f32[6,8,32,128]{3,2,1,0:T(8,128)S(1)}, f32[6,8,32,128]{3,2,1,0:T(8,128)S(1)}, u32[]{:S(2)}, u32[]{:S(2)}) collective-permute-start(f32[6,8,32,128]{3,2,1,0:T(8,128)S(1)} %get-tuple-element.29.refs_0_), channel_id=1, source_target_pairs={{0,4},{4,8},{8,12},{12,16},{16,20},{20,24},{24,28},{28,32},{32,36}... | collective-permute-start | bytes 2359304 | tf_op jit(solution)/shard_map/ppermute | solution.py:332
  181.6 24.7 %collective-permute-start.29 = (f32[6,8,32,128]{3,2,1,0:T(8,128)S(1)}, f32[6,8,32,128]{3,2,1,0:T(8,128)S(1)}, u32[]{:S(2)}, u32[]{:S(2)}) collective-permute-start(f32[6,8,32,128]{3,2,1,0:T(8,128)S(1)} %get-tuple-element.29.refs_0_), channel_id=1, source_target_pairs={{0,124},{4,0},{8,4},{12,8},{16,12},{20,16},{24,20},{28,24},{32,28}... | collective-permute-start | bytes 2359304 | tf_op jit(solution)/shard_map/ppermute | solution.py:332
  186.8 6.1 %collective-permute-start.24 = (f32[6,8,8,128]{3,2,1,0:T(8,128)S(1)}, f32[6,8,8,128]{3,2,1,0:T(8,128)S(1)}, u32[]{:S(2)}, u32[]{:S(2)}) collective-permute-start(f32[6,8,8,128]{3,2,1,0:T(8,128)S(1)} %get-tuple-element.30), channel_id=1, source_target_pairs={{0,1},{1,2},{2,3},{3,0},{4,5},{5,6},{6,7},{7,4},{8,9},{9,10},{10,1... | collective-permute-start | bytes 589832 | tf_op jit(solution)/shard_map/ppermute | solution.py:332
  189.4 8.6 %collective-permute-start.25 = (f32[6,8,8,128]{3,2,1,0:T(8,128)S(1)}, f32[6,8,8,128]{3,2,1,0:T(8,128)S(1)}, u32[]{:S(2)}, u32[]{:S(2)}) collective-permute-start(f32[6,8,8,128]{3,2,1,0:T(8,128)S(1)} %get-tuple-element.31), channel_id=1, source_target_pairs={{0,3},{1,0},{2,1},{3,2},{4,7},{5,4},{6,5},{7,6},{8,11},{9,8},{10,9... | collective-permute-start | bytes 589832 | tf_op jit(solution)/shard_map/ppermute | solution.py:332
  192.9 8.4 %collective-permute-start.27 = (f32[6,8,8,128]{3,2,1,0:T(8,128)S(1)}, f32[6,8,8,128]{3,2,1,0:T(8,128)S(1)}, u32[]{:S(2)}, u32[]{:S(2)}) collective-permute-start(f32[6,8,8,128]{3,2,1,0:T(8,128)S(1)} %collective-permute-done.24.refs_1_), channel_id=1, source_target_pairs={{0,4},{4,8},{8,12},{12,16},{16,20},{20,24},{24,28},{28,32},{32,36}... | collective-permute-start | bytes 589832 | tf_op jit(solution)/shard_map/ppermute | solution.py:332
  192.9 13.5 %collective-permute-start.30 = (f32[6,8,8,128]{3,2,1,0:T(8,128)S(1)}, f32[6,8,8,128]{3,2,1,0:T(8,128)S(1)}, u32[]{:S(2)}, u32[]{:S(2)}) collective-permute-start(f32[6,8,8,128]{3,2,1,0:T(8,128)S(1)} %collective-permute-done.24.refs_1_), channel_id=1, source_target_pairs={{0,124},{4,0},{8,4},{12,8},{16,12},{20,16},{24,20},{28,24},{32,28}... | collective-permute-start | bytes 589832 | tf_op jit(solution)/shard_map/ppermute | solution.py:332
  197.9 8.4 %collective-permute-start.28 = (f32[6,8,8,128]{3,2,1,0:T(8,128)S(1)}, f32[6,8,8,128]{3,2,1,0:T(8,128)S(1)}, u32[]{:S(2)}, u32[]{:S(2)}) collective-permute-start(f32[6,8,8,128]{3,2,1,0:T(8,128)S(1)} %collective-permute-done.25.refs_2_), channel_id=1, source_target_pairs={{0,4},{4,8},{8,12},{12,16},{16,20},{20,24},{24,28},{28,32},{32,36}... | collective-permute-start | bytes 589832 | tf_op jit(solution)/shard_map/ppermute | solution.py:332
  201.3 5.1 %collective-permute-start.31 = (f32[6,8,8,128]{3,2,1,0:T(8,128)S(1)}, f32[6,8,8,128]{3,2,1,0:T(8,128)S(1)}, u32[]{:S(2)}, u32[]{:S(2)}) collective-permute-start(f32[6,8,8,128]{3,2,1,0:T(8,128)S(1)} %collective-permute-done.25.refs_2_), channel_id=1, source_target_pairs={{0,124},{4,0},{8,4},{12,8},{16,12},{20,16},{24,20},{28,24},{32,28}... | collective-permute-start | bytes 589832 | tf_op jit(solution)/shard_map/ppermute | solution.py:332
  226.0 0.7 copy-start.4
  226.8 33.4 %collective-permute-start.34 = (f32[6,8,32,128]{3,2,1,0:T(8,128)S(1)}, f32[6,8,32,128]{3,2,1,0:T(8,128)}, u32[]{:S(2)}, u32[]{:S(2)}) collective-permute-start(f32[6,8,32,128]{3,2,1,0:T(8,128)S(1)} %get-tuple-element.32.refs_0_), channel_id=1, source_target_pairs={{0,4},{4,8},{8,12},{12,16},{16,20},{20,24},{24,28},{28,32},{32,36}... | collective-permute-start | bytes 2359304 | tf_op jit(solution)/shard_map/ppermute | solution.py:332
  226.8 33.4 %collective-permute-start.37 = (f32[6,8,32,128]{3,2,1,0:T(8,128)S(1)}, f32[6,8,32,128]{3,2,1,0:T(8,128)}, u32[]{:S(2)}, u32[]{:S(2)}) collective-permute-start(f32[6,8,32,128]{3,2,1,0:T(8,128)S(1)} %get-tuple-element.32.refs_0_), channel_id=1, source_target_pairs={{0,124},{4,0},{8,4},{12,8},{16,12},{20,16},{24,20},{28,24},{32,28}... | collective-permute-start | bytes 2359304 | tf_op jit(solution)/shard_map/ppermute | solution.py:332
  231.8 7.0 %collective-permute-start.32 = (f32[6,8,8,128]{3,2,1,0:T(8,128)S(1)}, f32[6,8,8,128]{3,2,1,0:T(8,128)}, u32[]{:S(2)}, u32[]{:S(2)}) collective-permute-start(f32[6,8,8,128]{3,2,1,0:T(8,128)S(1)} %get-tuple-element.33), channel_id=1, source_target_pairs={{0,1},{1,2},{2,3},{3,0},{4,5},{5,6},{6,7},{7,4},{8,9},{9,10},{10,1... | collective-permute-start | bytes 589832 | tf_op jit(solution)/shard_map/ppermute | solution.py:332
  235.2 13.6 %collective-permute-start.33 = (f32[6,8,8,128]{3,2,1,0:T(8,128)}, f32[6,8,8,128]{3,2,1,0:T(8,128)}, u32[]{:S(2)}, u32[]{:S(2)}) collective-permute-start(f32[6,8,8,128]{3,2,1,0:T(8,128)} %get-tuple-element.34), channel_id=1, source_target_pairs={{0,3},{1,0},{2,1},{3,2},{4,7},{5,4},{6,5},{7,6},{8,11},{9,8},{10,9... | collective-permute-start | bytes 589832 | tf_op jit(solution)/shard_map/ppermute | solution.py:332
  238.8 10.0 %collective-permute-start.35 = (f32[6,8,8,128]{3,2,1,0:T(8,128)}, f32[6,8,8,128]{3,2,1,0:T(8,128)}, u32[]{:S(2)}, u32[]{:S(2)}) collective-permute-start(f32[6,8,8,128]{3,2,1,0:T(8,128)} %collective-permute-done.32.refs_1_), channel_id=1, source_target_pairs={{0,4},{4,8},{8,12},{12,16},{16,20},{20,24},{24,28},{28,32},{32,36}... | collective-permute-start | bytes 589832 | tf_op jit(solution)/shard_map/ppermute | solution.py:332
  243.4 49.1 %copy-start.18 = (s32[1024]{0:T(1024)S(1)}, s32[1024]{0:T(1024)}, u32[]{:S(2)}) copy-start(s32[1024]{0:T(1024)} %param.13) | copy-start | bytes 12292
  243.7 15.7 %collective-permute-start.38 = (f32[6,8,8,128]{3,2,1,0:T(8,128)}, f32[6,8,8,128]{3,2,1,0:T(8,128)S(1)}, u32[]{:S(2)}, u32[]{:S(2)}) collective-permute-start(f32[6,8,8,128]{3,2,1,0:T(8,128)} %collective-permute-done.32.refs_1_), channel_id=1, source_target_pairs={{0,124},{4,0},{8,4},{12,8},{16,12},{20,16},{24,20},{28,24},{32,28}... | collective-permute-start | bytes 589832 | tf_op jit(solution)/shard_map/ppermute | solution.py:332
  248.8 10.6 %collective-permute-start.36 = (f32[6,8,8,128]{3,2,1,0:T(8,128)}, f32[6,8,8,128]{3,2,1,0:T(8,128)S(1)}, u32[]{:S(2)}, u32[]{:S(2)}) collective-permute-start(f32[6,8,8,128]{3,2,1,0:T(8,128)} %collective-permute-done.33.refs_2_), channel_id=1, source_target_pairs={{0,4},{4,8},{8,12},{12,16},{16,20},{20,24},{24,28},{28,32},{32,36}... | collective-permute-start | bytes 589832 | tf_op jit(solution)/shard_map/ppermute | solution.py:332
  248.9 10.6 %collective-permute-start.39 = (f32[6,8,8,128]{3,2,1,0:T(8,128)}, f32[6,8,8,128]{3,2,1,0:T(8,128)S(1)}, u32[]{:S(2)}, u32[]{:S(2)}) collective-permute-start(f32[6,8,8,128]{3,2,1,0:T(8,128)} %collective-permute-done.33.refs_2_), channel_id=1, source_target_pairs={{0,124},{4,0},{8,4},{12,8},{16,12},{20,16},{24,20},{28,24},{32,28}... | collective-permute-start | bytes 589832 | tf_op jit(solution)/shard_map/ppermute | solution.py:332
  259.4 0.7 copy-start.13
  260.1 0.9 copy-start.14
  281.9 0.9 copy-start.15
  283.8 13.2 %copy-start.16 = (s32[1024,1]{0,1:T(1,128)S(1)}, s32[1024,1]{0,1:T(1,128)}, u32[]{:S(2)}) copy-start(s32[1024,1]{0,1:T(1,128)} %param.14) | copy-start | bytes 12292
  283.9 13.0 %collective-permute-start.42 = (f32[96,128]{1,0:T(8,128)S(1)}, f32[96,128]{1,0:T(8,128)S(1)}, u32[]{:S(2)}, u32[]{:S(2)}) collective-permute-start(f32[96,128]{1,0:T(8,128)S(1)} %constant_dynamic-update-slice_fusion), channel_id=1, source_target_pairs={{0,3},{1,0},{2,1},{3,2},{4,7},{5,4},{6,5},{7,6},{8,11},{9,8},{10,9... | collective-permute-start | bytes 147464 | tf_op jit(solution)/shard_map/ppermute | solution.py:332
  287.2 9.7 %collective-permute-start.41 = (f32[96,128]{1,0:T(8,128)S(1)}, f32[96,128]{1,0:T(8,128)S(1)}, u32[]{:S(2)}, u32[]{:S(2)}) collective-permute-start(f32[96,128]{1,0:T(8,128)S(1)} %constant_dynamic-update-slice_fusion), channel_id=1, source_target_pairs={{0,2},{1,3},{2,0},{3,1},{4,6},{5,7},{6,4},{7,5},{8,10},{9,11},{10,... | collective-permute-start | bytes 147464 | tf_op jit(solution)/shard_map/ppermute | solution.py:332
  290.0 7.0 %collective-permute-start.40 = (f32[96,128]{1,0:T(8,128)S(1)}, f32[96,128]{1,0:T(8,128)S(1)}, u32[]{:S(2)}, u32[]{:S(2)}) collective-permute-start(f32[96,128]{1,0:T(8,128)S(1)} %constant_dynamic-update-slice_fusion), channel_id=1, source_target_pairs={{0,1},{1,2},{2,3},{3,0},{4,5},{5,6},{6,7},{7,4},{8,9},{9,10},{10,1... | collective-permute-start | bytes 147464 | tf_op jit(solution)/shard_map/ppermute | solution.py:332
Sparse Core Ops, SparseCore 0:
  19.7 86.7 all-gather.1
where the time goes:
time: 319 us; the launch traced here: 318 us
  Pallas kernels  122 us (38%)
  starting transfers between devices  81.5 us (26%)
  waiting for transfers between devices  50.8 us (16%)
  local copies, waits for them, and re-layouts  43.1 us (14%)
  between operations  14.4 us (5%)
  other arithmetic  5.65 us (2%)
    pallas_call x5, Pallas kernels, run_grid(): pl.pallas_call(functools.partial(grid_kernel, first, snap_step), out_shap...  98.1 us
    ppermute x43, starting transfers between devices, ring(): lax.ppermute(value, axis, [(i, (i + shift) % count) for i in range(count)])  81.5 us
    ppermute x43, waiting for transfers between devices, ring(): lax.ppermute(value, axis, [(i, (i + shift) % count) for i in range(count)])  50.7 us
    unnamed x42, local copies, waits for them, and re-layouts  14 us
    pallas_call x1, Pallas kernels, building_states(): pl.pallas_call(building_kernel, out_shape=jax.ShapeDtypeStruct((count, wi...  13.9 us
    pallas_call x1, Pallas kernels, responses(): pl.pallas_call(response_kernel, out_shape=jax.ShapeDtypeStruct((arch, COU...  10.4 us
    concatenate x8, local copies, waits for them, and re-layouts, per_device(): jnp.concatenate([displacement, previous, shear_coef[None] / 12.0, bulk_co...  9.45 us
    slice x4, local copies, waits for them, and re-layouts, per_device(): ground = result[-1][..., ::NZ]  8.29 us
  transfers between devices with their start and end apart: 44, of which 15 were waited for; matrix products, arithmetic and copies ran while one was open for 11% of the time, Pallas kernels for 31%

commit v1 on v0

v1 whole, which is shorter than its diff:
```python
import functools

import jax
import jax.numpy as jnp
import numpy as np
from jax import lax
from jax.experimental import pallas as pl
from jax.experimental.pallas import tpu as pltpu
from jax.sharding import PartitionSpec as P

COUPLINGS = 4
EVERY = 5
SUB = 6
NZ = 32
CX = 8
CY = 128
GROUPS = 4
ROWS = CY // GROUPS
STEPS = 4
X0 = 2 * STEPS + 2
XE = 2 * X0 + CX
TILES_Y = (2, 1, 2, 1, 1)
R0 = 8 * max(TILES_Y) + 8
RE = 2 * R0 + ROWS
CHUNK = 4
VMEM = pl.BlockSpec(memory_space=pltpu.VMEM)
SMEM = pl.BlockSpec(memory_space=pltpu.SMEM)


def depth_weights():
    matrix = np.zeros((128, 256), np.float32)
    for lane in range(128):
        base, z = lane // NZ * NZ, lane % NZ
        for k, offset in enumerate(range(-2, 3)):
            source = abs(z + offset)
            if source < NZ:
                matrix[base + source, lane] += (-1, 16, -30, 16, -1)[k]
                matrix[base + source, 128 + lane] += (1, -8, 0, 8, -1)[k]
    return np.concatenate([matrix, matrix])


def block_of_lanes(shape):
    return lax.broadcasted_iota(jnp.int32, shape, len(shape) - 1) // NZ


def turn(value, blocks):
    shift = NZ * (blocks % GROUPS)
    return pltpu.roll(value, shift, 1) if shift else value


def pick_block(values, j):
    lanes = block_of_lanes(values[0].shape)
    result = turn(values[0], 0 - j)
    for i in range(1, GROUPS):
        result = jnp.where(lanes == i, turn(values[i], i - j), result)
    return result


def advance(step, tiles_y, field, former, shear, bulk, scratch, weights_ref):
    second_z, part_x, part_y, first_zx, first_zy = scratch
    halo = 8 * tiles_y
    row_a, tiles_a = R0 - halo - 2 + 2 * step, -(-(ROWS + 2 * halo + 4 - 4 * step) // 8)
    row_b, tiles_b = R0 - halo + 2 * step, -(-(ROWS + 2 * halo - 4 * step) // 8)
    start_a, count_a = 2 * step, XE - 4 * step
    start_b, count_b = start_a + 2, count_a - 4
    height = 8 * tiles_a
    window = pl.ds(row_a, height)

    def firsts(chunk, carry):
        x = start_a + CHUNK * chunk
        values = jnp.concatenate(
            [field[c, x + i, window, :] for c in range(3) for i in range(CHUNK)]
        )
        high = values.astype(jnp.bfloat16)
        low = (values - high.astype(jnp.float32)).astype(jnp.bfloat16)
        along_z = jnp.dot(
            jnp.concatenate([high, low], axis=1),
            weights_ref[...],
            preferred_element_type=jnp.float32,
        )
        for i in range(CHUNK):
            for c in range(3):
                at = (CHUNK * c + i) * height
                second_z[c, x + i, window, :] = along_z[at : at + height, 0:128]
            at = i * height
            first_zx[x + i, window, :] = along_z[at : at + height, 128:256]
            at = (CHUNK + i) * height
            first_zy[x + i, window, :] = along_z[at : at + height, 128:256]
        for k in range(tiles_a):
            r = row_a + 8 * k
            rows = pl.ds(r, 8)
            across = [field[0, x + d, rows, :] for d in range(-2, CHUNK + 2)]
            for i in range(CHUNK):
                at = lambda d: field[1, x + i, pl.ds(r + d, 8), :]
                first_y = 8.0 * (at(1) - at(-1)) - (at(2) - at(-2))
                first_x = 8.0 * (across[i + 3] - across[i + 1]) - (across[i + 4] - across[i])
                place = (2 * CHUNK + i) * height + 8 * k
                first_z = along_z[place : place + 8, 128:256]
                part_x[x + i, rows, :] = first_y + first_z
                part_y[x + i, rows, :] = first_x + first_z
        return carry

    def update(chunk, carry):
        x = start_b + CHUNK * chunk
        for k in range(tiles_b):
            r = row_b + 8 * k
            rows = pl.ds(r, 8)

            def first_x(ref):
                across = [ref[x + d, rows, :] for d in range(-2, CHUNK + 2)]
                return [
                    8.0 * (across[i + 3] - across[i + 1]) - (across[i + 4] - across[i])
                    for i in range(CHUNK)
                ]

            def first_y(ref, i):
                at = lambda d: ref[x + i, pl.ds(r + d, 8), :]
                return 8.0 * (at(1) - at(-1)) - (at(2) - at(-2))

            for c in range(3):
                across = [field[c, x + d, rows, :] for d in range(-2, CHUNK + 2)]
                if c == 0:
                    mixed = first_x(part_x)
                elif c == 1:
                    mixed = [first_y(part_y, i) for i in range(CHUNK)]
                else:
                    mixed = [
                        value + first_y(first_zy, i)
                        for i, value in enumerate(first_x(first_zx))
                    ]
                for i in range(CHUNK):
                    at = lambda d: field[c, x + i, pl.ds(r + d, 8), :]
                    centre = across[i + 2]
                    d_x = 16.0 * (across[i + 3] + across[i + 1]) - (across[i + 4] + across[i])
                    d_y = 16.0 * (at(1) + at(-1)) - (at(2) + at(-2))
                    d_z = second_z[c, x + i, rows, :]
                    own = (d_x - 30.0 * centre, d_y - 30.0 * centre, d_z)[c]
                    laplacian = (d_x + d_y) + (d_z - 60.0 * centre)
                    change = shear[x + i, rows, :] * laplacian + bulk[x + i, rows, :] * (
                        own + (1.0 / 12.0) * mixed[i]
                    )
                    former[c, x + i, rows, :] = (
                        2.0 * centre - former[c, x + i, rows, :]
                    ) + change
        return carry

    lax.fori_loop(0, count_a // CHUNK, firsts, 0)
    lax.fori_loop(0, count_b // CHUNK, update, 0)


def place_block(own, halo, halo_from, tiles_y, exists, x_from, targets):
    lanes = block_of_lanes((8, 128))
    here, from_low, from_high = exists

    def keep(flag, value):
        return value if flag is None else jnp.where(flag, value, 0.0)

    def columns(q, carry):
        for f, target in enumerate(targets):
            low, high = [
                [
                    keep(
                        (from_low, from_high)[side],
                        halo[
                            f,
                            pl.ds(
                                pl.multiple_of(
                                    halo_from + 8 * ((2 * side + q) * tiles_y + j), 8
                                ),
                                8,
                            ),
                            :,
                        ],
                    )
                    for j in range(tiles_y)
                ]
                for side in range(2)
            ]
            for i in range(4):
                x = 4 * q + i
                first = pl.multiple_of(ROWS * x, 8)
                tiles = [
                    keep(here, own[f, pl.ds(first + 8 * k, 8), :]) for k in range(ROWS // 8)
                ]
                for k in range(ROWS // 8):
                    target[x_from + x, pl.ds(R0 + 8 * k, 8), :] = tiles[k]
                for j in range(tiles_y):
                    target[x_from + x, pl.ds(R0 + 8 * (j - tiles_y), 8), :] = jnp.where(
                        lanes == 0,
                        turn(low[j], 0 - i),
                        turn(tiles[ROWS // 8 - tiles_y + j], 1),
                    )
                    target[x_from + x, pl.ds(R0 + ROWS + 8 * j, 8), :] = jnp.where(
                        lanes == GROUPS - 1,
                        turn(high[j], GROUPS - 1 - i),
                        turn(tiles[j], GROUPS - 1),
                    )
        return carry

    lax.fori_loop(0, CX // 4, columns, 0)


def grid_kernel(block, merged, snap_step, edge, weights_ref, *refs):
    first, last = block == 0, block == len(TILES_Y) - 1
    tiles_y = TILES_Y[block]
    refs = list(refs)
    take = lambda n: [refs.pop(0) for _ in range(n)]
    blocks = [take(1 if merged else 2) for _ in range(3)]
    if first:
        sends = take(1 if TILES_Y[1] < tiles_y else 3)
        shear, bulk = take(2)
    else:
        shear, bulk = take(2)
        sends = take(1) if last or TILES_Y[block + 1] < tiles_y else take(3)
    snap = take(1)[0] if snap_step is not None else None
    fields = take(2)

    low_here, high_here = edge[2] == 1, edge[3] == 1
    for i, arrays in enumerate(blocks):
        here = (None, edge[0] == 1, edge[1] == 1)[i]
        sides = [
            side if here is None else jnp.logical_and(here, side)
            for side in (low_here, high_here)
        ]
        targets = [fields[f // 3].at[f % 3] for f in range(6)]
        if first:
            targets = targets + [shear, bulk]
        place_block(
            arrays[0],
            arrays[-1],
            CX * ROWS if merged else 0,
            tiles_y,
            (here, *sides),
            (X0, X0 - CX, X0 + CX)[i],
            targets,
        )

    now, before = fields
    for step in range(1, STEPS + 1):
        advance(step, tiles_y, now, before, shear, bulk, refs, weights_ref)
        now, before = before, now
        if step == snap_step and not last:
            for x in range(CX):
                snap[:, pl.ds(ROWS * x, ROWS), :] = now[:, X0 + x, pl.ds(R0, ROWS), :]
    if last:
        whole = sends[0]
        for c in range(3):
            for q in range(CX // 4):
                columns = [now[c, X0 + 4 * q + i, pl.ds(R0, ROWS), :] for i in range(4)]
                grid = jnp.concatenate([pick_block(columns, g) for g in range(GROUPS)]).T
                for i in range(4):
                    x = 4 * q + i
                    rows = grid[NZ * i : NZ * i + NZ]
                    whole[pl.ds(c * NZ * CX + x, NZ, stride=CX), :] = rows
                    snap[CX * c + x : CX * c + x + 1, :] = rows[0:1]
        return
    for f in range(6):
        source = (now, before)[f // 3].at[f % 3]
        for x in range(CX):
            sends[0][f, pl.ds(ROWS * x, ROWS), :] = source[X0 + x, pl.ds(R0, ROWS), :]
        if len(sends) == 1:
            depth, far = tiles_y - 1, sends[0]
            spots = ((R0 - 8 * depth, 0), (R0 + ROWS, GROUPS - 1))
            starts = (CX * ROWS, CX * ROWS + 16 * depth)
            outs = (far, far)
        else:
            depth = TILES_Y[block + 1]
            spots = ((R0 + ROWS - 8 * depth, GROUPS - 1), (R0, 0))
            starts, outs = (0, 0), sends[1:]
        for (row, group), start, out in zip(spots, starts, outs):
            for q in range(CX // 4):
                columns = [source[X0 + 4 * q + i, pl.ds(row, 8 * depth), :] for i in range(4)]
                out[f, pl.ds(start + 8 * depth * q, 8 * depth), :] = pick_block(columns, group)


def run_grid(block, snap_step, edge, weights, blocks, coefs):
    shape = lambda *s: jax.ShapeDtypeStruct(s, jnp.float32)
    last = block == len(TILES_Y) - 1
    merged = len(blocks[0]) == 1
    if last:
        outs = [shape(3 * NZ * CX, CY)]
    elif TILES_Y[block + 1] < TILES_Y[block]:
        outs = [shape(6, CX * ROWS + 32 * (TILES_Y[block] - 1), 128)]
    else:
        outs = [shape(6, CX * ROWS, 128)] + [shape(6, 16 * TILES_Y[block + 1], 128)] * 2
    operands = [edge, weights] + [array for arrays in blocks for array in arrays]
    if block == 0:
        outs += [shape(XE, RE, 128)] * 2
    else:
        operands += list(coefs)
    if snap_step is not None:
        outs.append(shape(3 * CX, CY) if last else shape(3, CX * ROWS, 128))
    field = pltpu.VMEM((3, XE, RE, 128), jnp.float32)
    plane = pltpu.VMEM((XE, RE, 128), jnp.float32)
    return pl.pallas_call(
        functools.partial(grid_kernel, block, merged, snap_step),
        out_shape=outs,
        in_specs=[SMEM] + [VMEM] * (len(operands) - 1),
        out_specs=[VMEM] * len(outs),
        scratch_shapes=[field, field, field, plane, plane, plane, plane],
        compiler_params=pltpu.CompilerParams(vmem_limit_bytes=48 << 20),
        cost_estimate=pl.CostEstimate(
            flops=40_000_000, bytes_accessed=8 << 20, transcendentals=0
        ),
        name="grid_steps",
    )(*operands)


def arrange_kernel(now, before, shear, bulk, own, low, high):
    depth = 8 * TILES_Y[0]
    for f in range(8):
        ref, base = ((now, 256 * f), (before, 256 * (f - 3)), (shear, 0), (bulk, 0))[
            f // 3 if f < 6 else f - 4
        ]
        for q in range(CX // 4):
            values = [ref[pl.ds(base + 4 * q + i, NZ, stride=CX), :] for i in range(4)]
            grid = jnp.concatenate(values).T
            if f >= 6:
                grid = grid * (1.0 / 12.0)
            low[f, pl.ds(depth * q, depth), :] = grid[CY - depth : CY]
            high[f, pl.ds(depth * q, depth), :] = grid[0:depth]
            groups = [grid[ROWS * g : ROWS * g + ROWS] for g in range(GROUPS)]
            for i in range(4):
                own[f, pl.ds(ROWS * (4 * q + i), ROWS), :] = pick_block(groups, i)


def arrange(displacement, previous, shear_coef, bulk_coef):
    shape = lambda *s: jax.ShapeDtypeStruct(s, jnp.float32)
    side = shape(8, 16 * TILES_Y[0], 128)
    flat = [a.reshape(-1, CY) for a in (displacement, previous, shear_coef, bulk_coef)]
    return pl.pallas_call(
        arrange_kernel,
        out_shape=[shape(8, CX * ROWS, 128), side, side],
        in_specs=[VMEM] * 4,
        out_specs=[VMEM] * 3,
        compiler_params=pltpu.CompilerParams(vmem_limit_bytes=24 << 20),
        cost_estimate=pl.CostEstimate(
            flops=1_000_000, bytes_accessed=4 << 20, transcendentals=0
        ),
        name="arrange",
    )(*flat)


def response_kernel(transition, forcing, out, state, total):
    arch = transition.shape[0]
    state[...] = jnp.zeros_like(state)
    out[...] = jnp.zeros_like(out)
    for a in range(arch):
        state[a, 0:3, :] = forcing[a]

    def one(j, carry):
        for a in range(arch):
            now = state[a]
            total[a] = total[a] + now
            high = now.astype(jnp.bfloat16)
            low = (now - high.astype(jnp.float32)).astype(jnp.bfloat16)
            product = lax.dot_general(
                jnp.concatenate([high, low], axis=0),
                transition[a],
                (((1,), (1,)), ((), ())),
                preferred_element_type=jnp.float32,
            )
            state[a] = product[0:8] + product[8:16]
        return carry

    for group in range(COUPLINGS):
        moment = COUPLINGS - 1 - group
        total[...] = jnp.zeros_like(total)
        lax.fori_loop(0, SUB, one, 0)
        for a in range(arch):
            for c in range(3):
                for h in range(2):
                    row = 2 * c + h
                    out[a, moment, row : row + 1, :] = total[
                        a, c : c + 1, 128 * h : 128 * h + 128
                    ]
            if group < COUPLINGS - 1:
                scale = jnp.maximum(jnp.max(jnp.abs(state[a]), keepdims=True), 1.0)
                state[a] = state[a] / scale
                out[a, moment, 6:7, :] = jnp.broadcast_to(scale, (1, 128))


def responses(transition, forcing):
    arch, width = transition.shape[0], transition.shape[1]
    return pl.pallas_call(
        response_kernel,
        out_shape=jax.ShapeDtypeStruct((arch, COUPLINGS, 8, 128), jnp.float32),
        in_specs=[VMEM, VMEM],
        out_specs=VMEM,
        scratch_shapes=[pltpu.VMEM((arch, 8, width), jnp.float32)] * 2,
        compiler_params=pltpu.CompilerParams(vmem_limit_bytes=24 << 20),
        cost_estimate=pl.CostEstimate(
            flops=20_000_000, bytes_accessed=2 << 20, transcendentals=0
        ),
        name="responses",
    )(transition, forcing)


def building_kernel(kinds, place, across, surface, table, out, ground):
    count = out.shape[0]
    cells = surface.shape[0] * CY
    picks = (lax.broadcasted_iota(jnp.int32, (cells, count), 0) == place[...]).astype(jnp.bfloat16)
    values = jnp.concatenate([surface[j] for j in range(surface.shape[0])], axis=1)
    high = values.astype(jnp.bfloat16)
    rest = values - high.astype(jnp.float32)
    low = rest.astype(jnp.bfloat16)
    least = (rest - low.astype(jnp.float32)).astype(jnp.bfloat16)
    picked = jnp.dot(
        jnp.concatenate([high, low, least], axis=0), picks, preferred_element_type=jnp.float32
    )
    n = values.shape[0]
    picked = picked[0:n] + picked[n : 2 * n] + picked[2 * n : 3 * n]
    here = lax.broadcasted_iota(jnp.int32, (CX, count), 0) == across[...]
    row = lax.broadcasted_iota(jnp.int32, (8, count), 0)
    for m in range(COUPLINGS):
        rows = []
        for c in range(3):
            k = 3 * m + c
            value = jnp.where(here, picked[CX * k : CX * k + CX], 0.0)
            rows.append(jnp.sum(value, axis=0, keepdims=True))
        ground[m] = jnp.where(
            row < 2, rows[0], jnp.where(row < 4, rows[1], jnp.where(row < 6, rows[2], 0.0))
        )

    def tile(t, carry):
        base = pl.multiple_of(t * 128, 128)
        motion = [ground[m, :, pl.ds(base, 128)] for m in range(COUPLINGS)]
        slot = lax.broadcasted_iota(jnp.int32, (8, 128), 0)
        for eight in range(16):
            halves = [jnp.zeros((8, 128), jnp.float32)] * 2
            for k in range(8):
                i = 8 * eight + k
                kind = kinds[base + i]
                total = None
                for m in range(COUPLINGS):
                    term = table[kind, m] * jnp.broadcast_to(motion[m][:, i : i + 1], (8, 128))
                    if total is None:
                        total = term
                    else:
                        scale = jnp.broadcast_to(table[kind, m, 6:7, :], (8, 128))
                        total = total * scale + term
                total = total + pltpu.roll(total, 4, 0)
                total = total + pltpu.roll(total, 2, 0)
                other = pltpu.roll(total, 1, 0)
                pair = (total, other) if k % 2 == 0 else (other, total)
                halves = [jnp.where(slot == k, new, old) for new, old in zip(pair, halves)]
            rows = pl.ds(base + 8 * eight, 8)
            out[rows, 0:128] = halves[0]
            out[rows, 128:256] = halves[1]
        return carry

    lax.fori_loop(0, count // 128, tile, 0)


def building_states(kinds, place, across, surface, table, width):
    count = kinds.shape[0]
    return pl.pallas_call(
        building_kernel,
        out_shape=jax.ShapeDtypeStruct((count, width), jnp.float32),
        in_specs=[SMEM] + [VMEM] * 4,
        out_specs=VMEM,
        scratch_shapes=[pltpu.VMEM((COUPLINGS, 8, count), jnp.float32)],
        compiler_params=pltpu.CompilerParams(vmem_limit_bytes=50 << 20),
        cost_estimate=pl.CostEstimate(
            flops=20_000_000, bytes_accessed=18 << 20, transcendentals=0
        ),
        name="buildings",
    )(kinds, place[None, :], across[None, :], surface, table)


def ring(value, axis, shift):
    count = lax.axis_size(axis)
    return lax.ppermute(value, axis, [(i, (i + shift) % count) for i in range(count)])


def exchange(own, low=None, high=None):
    if low is None:
        return [[own]] + [[ring(own, "slab", shift)] for shift in (1, -1)]
    sides = jnp.concatenate([ring(low, "gy", 1), ring(high, "gy", -1)], axis=1)
    return [[own, sides]] + [
        [ring(own, "slab", shift), ring(sides, "slab", shift)] for shift in (1, -1)
    ]


def per_device(
    displacement, previous, shear_coef, bulk_coef, cell_index, archetype_id, transition, forcing
):
    width = transition.shape[1]
    slab, gy = lax.axis_index("slab"), lax.axis_index("gy")
    slabs, strips = lax.axis_size("slab"), lax.axis_size("gy")
    edge = jnp.stack([slab > 0, slab < slabs - 1, gy > 0, gy < strips - 1]).astype(jnp.int32)
    weights = jnp.asarray(depth_weights(), jnp.bfloat16)

    blocks = exchange(*arrange(displacement, previous, shear_coef, bulk_coef))
    table = lax.all_gather(responses(transition, forcing), ("slab", "gy"), axis=0, tiled=True)

    snaps = []
    coefs = None
    count = len(TILES_Y)
    for block in range(count):
        snap_step = next(
            (s for s in range(1, STEPS + 1) if (block * STEPS + s) % EVERY == 0), None
        )
        result = run_grid(block, snap_step, edge, weights, blocks, coefs)
        sends = 3 if block < count - 1 and TILES_Y[block + 1] >= TILES_Y[block] else 1
        if block == 0:
            coefs = result[sends : sends + 2]
        if block == count - 1:
            final = result[0].reshape(3, NZ, CX, CY)
            snaps.append(result[1])
        else:
            blocks = exchange(*result[:sends])
            if snap_step is not None:
                ground = result[-1].reshape(3, CX, ROWS, 128)[..., ::NZ]
                snaps.append(ground.transpose(0, 1, 3, 2).reshape(3 * CX, CY))

    mine = jnp.concatenate(snaps)
    surface = jnp.stack([mine] + [ring(mine, "gy", shift) for shift in range(1, strips)])
    columns = strips * CY
    along_y = cell_index % columns
    across = cell_index // columns - slab * CX
    place = (gy - along_y // CY) % strips * CY + along_y % CY
    states = building_states(archetype_id[:, 0], place, across, surface, table, width)
    return (final, states)


def solution(mesh):
    in_specs = (
        P(None, None, "slab", "gy"),
        P(None, None, "slab", "gy"),
        P(None, "slab", "gy"),
        P(None, "slab", "gy"),
        P(("slab", "gy")),
        P(("slab", "gy"), None),
        P(("slab", "gy"), None, None),
        P(("slab", "gy"), None, None),
    )
    out_specs = (P(None, None, "slab", "gy"), P(("slab", "gy"), None))
    return jax.shard_map(
        per_device, mesh=mesh, in_specs=in_specs, out_specs=out_specs, check_vma=False
    )
```

time: 319 us -> 231 us (0.72)
  Pallas kernels: 122 us -> 82.3 us
  starting transfers between devices: 81.5 us -> 52.1 us
  local copies, waits for them, and re-layouts: 43.1 us -> 19.3 us
  waiting for transfers between devices: 50.8 us -> 60.8 us
  other arithmetic: 5.65 us -> 0.12 us
    pallas_call x5 -> x6, Pallas kernels: 98.1 us -> 58.1 us  [the longest x5 56.9 us: run_grid(): pl.pallas_call(functools.partial(grid_kernel, block, merged, snap_step),...]
    ppermute x43 -> x25, starting transfers between devices: 81.5 us -> 52 us  [ring(): lax.ppermute(value, axis, [(i, (i + shift) % count) for i in range(count)])]
    ppermute x43 -> x25, waiting for transfers between devices: 50.7 us -> 60.8 us  [ring(): lax.ppermute(value, axis, [(i, (i + shift) % count) for i in range(count)])]
    concatenate x8 -> x3, local copies, waits for them, and re-layouts: 9.45 us -> 0.68 us  [exchange(): sides = jnp.concatenate([ring(low, 'gy', 1), ring(high, 'gy', -1)], axis=1)]
    reshape x3 -> x0, local copies, waits for them, and re-layouts: 5.83 us -> none  [the longest x1 3.72 us: per_device(): own = own.reshape(8, CX, ROWS, 128)]
    unnamed x42 -> x34, local copies, waits for them, and re-layouts: 14 us -> 9.32 us
    transpose x5 -> x0, local copies, waits for them, and re-layouts: 4.06 us -> none  [the longest x4 2.82 us: per_device(): snaps.append(ground.transpose(0, 1, 3, 2).reshape(3 * CX, CY))]
    transpose x1 -> x0, other arithmetic: 3.69 us -> none  [per_device(): own = stacked.reshape(8, NZ, CX, GROUPS, ROWS).transpose(0, 2, 4, 3, 1)]
  transfers between devices with their start and end apart: 44 -> 26, of which waited for: 15 -> 11; matrix products, arithmetic and copies ran while one was open for 11% -> 6% of each run, Pallas kernels for 31% -> 25%
where the time goes in v1:
time: 231 us; the launch traced here: 229 us
  Pallas kernels  82.3 us (36%)
  waiting for transfers between devices  60.8 us (26%)
  starting transfers between devices  52.1 us (23%)
  local copies, waits for them, and re-layouts  19.3 us (8%)
  between operations  14.3 us (6%)
    ppermute x25, waiting for transfers between devices, ring(): lax.ppermute(value, axis, [(i, (i + shift) % count) for i in range(count)])  60.8 us
    pallas_call x5, Pallas kernels, run_grid(): pl.pallas_call(functools.partial(grid_kernel, block, merged, snap_step),...  56.9 us
    ppermute x25, starting transfers between devices, ring(): lax.ppermute(value, axis, [(i, (i + shift) % count) for i in range(count)])  52 us
    pallas_call x1, Pallas kernels, building_states(): pl.pallas_call(building_kernel, out_shape=jax.ShapeDtypeStruct((count, wi...  13.9 us
    pallas_call x1, Pallas kernels, responses(): pl.pallas_call(response_kernel, out_shape=jax.ShapeDtypeStruct((arch, COU...  10.3 us
    unnamed x34, local copies, waits for them, and re-layouts  9.32 us
    slice x3, local copies, waits for them, and re-layouts, per_device(): ground = result[-1].reshape(3, CX, ROWS, 128)[..., ::NZ]  8.99 us
  transfers between devices with their start and end apart: 26, of which 11 were waited for; matrix products, arithmetic and copies ran while one was open for 6% of the time, Pallas kernels for 25%

profile of v1, /device:TPU:16, one launch (start us, length us, event | category | flops | bytes accessed | tf_op | source)
XLA Modules:
  0.0 228.9 jit_solution(2965384169238129068)
XLA Ops:
  7.2 0.0 all-gather.2.cloned.1.call-start
  7.2 0.8 copy.18.forcing
  8.0 0.0 copy-start.2
  8.0 1.2 copy-done.2
  9.2 10.3 %responses.1 = f32[8,4,8,128]{3,2,1,0:T(8,128)} custom-call(bf16[8,256,256]{2,1,0:T(8,128)(2,1)S(1)} %copy-done.2, f32[8,3,256]{2,1,0:T(4,128)S(1)} %copy.18.forcing), custom_call_target="tpu_custom_call" | custom-call | flops 20000000 | bytes 2097152 | tf_op jit(solution)/shard_map/responses/pallas_call | solution.py:385
  19.5 0.0 all-gather.2.cloned.1.call-update
  19.6 1.2 arrange.1
  20.8 0.1 collective-permute-start.2
  20.9 5.7 %collective-permute-start.4 = (f32[8,256,128]{2,1,0:T(8,128)S(1)}, f32[8,256,128]{2,1,0:T(8,128)S(1)}, u32[]{:S(2)}, u32[]{:S(2)}) collective-permute-start(f32[8,256,128]{2,1,0:T(8,128)S(1)} %get-tuple-element.20.refs_0_), channel_id=1, source_target_pairs={{0,124},{4,0},{8,4},{12,8},{16,12},{20,16},{24,20},{28,24},{32,28}... | collective-permute-start | bytes 3145736 | tf_op jit(solution)/shard_map/ppermute | solution.py:473
  26.6 1.3 collective-permute-start
  27.9 0.7 collective-permute-start.1
  28.6 2.9 %collective-permute-done = f32[8,32,128]{2,1,0:T(8,128)S(1)} collective-permute-done((f32[8,32,128]{2,1,0:T(8,128)S(1)}, f32[8,32,128]{2,1,0:T(8,128)S(1)}, u32[]{:S(2)}, u32[]{:S(2)}) %collective-permute-start) | collective-permute-done | bytes 131104 | tf_op jit(solution)/shard_map/ppermute | solution.py:473
  31.6 0.7 constant_dynamic-update-slice_fusion.1
  32.2 0.6 collective-permute-done.1
  32.9 0.7 constant_dynamic-update-slice_fusion.refs_1_
  33.5 5.1 %collective-permute-start.5 = (f32[8,64,128]{2,1,0:T(8,128)}, f32[8,64,128]{2,1,0:T(8,128)}, u32[]{:S(2)}, u32[]{:S(2)}) collective-permute-start(f32[8,64,128]{2,1,0:T(8,128)} %constant_dynamic-update-slice_fusion.refs_1_), channel_id=1, source_target_pairs={{0,124},{4,0},{8,4},{12,8},{16,12},{20,16},{24,20},{28,24},{32,28}... | collective-permute-start | bytes 786440 | tf_op jit(solution)/shard_map/ppermute | solution.py:473
  38.6 0.1 add_convert_fusion.edge
  38.7 4.8 %collective-permute-done.3.refs_3_ = f32[8,64,128]{2,1,0:T(8,128)} collective-permute-done((f32[8,64,128]{2,1,0:T(8,128)}, f32[8,64,128]{2,1,0:T(8,128)}, u32[]{:S(2)}, u32[]{:S(2)}) %collective-permute-start.3) | collective-permute-done | bytes 262176 | tf_op jit(solution)/shard_map/ppermute | solution.py:473
  43.5 0.0 copy-start.3
  43.5 1.0 copy-done.3
  44.5 1.2 copy-done.4
  45.7 13.3 %grid_steps.5 = (f32[6,288,128]{2,1,0:T(8,128)S(1)}, f32[28,80,128]{2,1,0:T(8,128)S(1)}, f32[28,80,128]{2,1,0:T(8,128)}) custom-call(s32[4]{0:T(128)S(1)} %add_convert_fusion.edge, bf16[256,256]{1,0:T(8,128)(2,1)S(1)} %copy-done.1, f32[8,256,128]{2,1,0:T(8,128)S(1)} %get-tuple-element.20.refs_0_, f32[8,64,128]{2,1,0:T(8,128)} %constant_dynamic-update-slice_fusion.refs_1_, ...), custom_call_target="tpu_custom_call" | custom-call | flops 40000000 | bytes 8388608 | tf_op jit(solution)/shard_map/grid_steps/pallas_call | solution.py:295
  59.0 5.1 %collective-permute-start.7 = (f32[6,288,128]{2,1,0:T(8,128)S(1)}, f32[6,288,128]{2,1,0:T(8,128)S(1)}, u32[]{:S(2)}, u32[]{:S(2)}) collective-permute-start(f32[6,288,128]{2,1,0:T(8,128)S(1)} %get-tuple-element.23.refs_0_), channel_id=1, source_target_pairs={{0,124},{4,0},{8,4},{12,8},{16,12},{20,16},{24,20},{28,24},{32,28}... | collective-permute-start | bytes 2654216 | tf_op jit(solution)/shard_map/ppermute | solution.py:473
  64.2 12.7 %collective-permute-done.6.refs_1_ = f32[6,288,128]{2,1,0:T(8,128)S(1)} collective-permute-done((f32[6,288,128]{2,1,0:T(8,128)S(1)}, f32[6,288,128]{2,1,0:T(8,128)S(1)}, u32[]{:S(2)}, u32[]{:S(2)}) %collective-permute-start.6) | collective-permute-done | bytes 884768 | tf_op jit(solution)/shard_map/ppermute | solution.py:473
  76.9 10.1 %grid_steps.6 = (f32[6,256,128]{2,1,0:T(8,128)S(1)}, f32[6,32,128]{2,1,0:T(8,128)S(1)}, f32[6,32,128]{2,1,0:T(8,128)S(1)}, f32[3,256,128]{2,1,0:T(8,128)S(1)}) custom-call(s32[4]{0:T(128)S(1)} %add_convert_fusion.edge, bf16[256,256]{1,0:T(8,128)(2,1)S(1)} %copy-done.1, f32[6,288,128]{2,1,0:T(8,128)S(1)} %get-tuple-element.23.refs_0_, ...), custom_call_target="tpu_custom_call" | custom-call | flops 40000000 | bytes 8388608 | tf_op jit(solution)/shard_map/grid_steps/pallas_call | solution.py:295
  87.0 0.1 collective-permute-start.10
  87.1 5.1 %collective-permute-start.12 = (f32[6,256,128]{2,1,0:T(8,128)S(1)}, f32[6,256,128]{2,1,0:T(8,128)S(1)}, u32[]{:S(2)}, u32[]{:S(2)}) collective-permute-start(f32[6,256,128]{2,1,0:T(8,128)S(1)} %get-tuple-element.26.refs_0_), channel_id=1, source_target_pairs={{0,124},{4,0},{8,4},{12,8},{16,12},{20,16},{24,20},{28,24},{32,28}... | collective-permute-start | bytes 2359304 | tf_op jit(solution)/shard_map/ppermute | solution.py:473
  92.1 1.2 collective-permute-start.8
  93.3 0.8 collective-permute-start.9
  94.2 4.7 %collective-permute-done.8 = f32[6,32,128]{2,1,0:T(8,128)S(1)} collective-permute-done((f32[6,32,128]{2,1,0:T(8,128)S(1)}, f32[6,32,128]{2,1,0:T(8,128)S(1)}, u32[]{:S(2)}, u32[]{:S(2)}) %collective-permute-start.8) | collective-permute-done | bytes 98336 | tf_op jit(solution)/shard_map/ppermute | solution.py:473
  98.8 1.2 collective-permute-done.9
  100.0 0.1 collective-permute-start.11
  100.1 5.1 %collective-permute-start.13 = (f32[6,64,128]{2,1,0:T(8,128)S(1)}, f32[6,64,128]{2,1,0:T(8,128)S(1)}, u32[]{:S(2)}, u32[]{:S(2)}) collective-permute-start(f32[6,64,128]{2,1,0:T(8,128)S(1)} %constant_dynamic-update-slice_fusion.2.refs_1_), channel_id=1, source_target_pairs={{0,124},{4,0},{8,4},{12,8},{16,12},{20,16},{24,20},{28,24},{32,28}... | collective-permute-start | bytes 589832 | tf_op jit(solution)/shard_map/ppermute | solution.py:473
  105.2 17.8 %collective-permute-done.11.refs_3_ = f32[6,64,128]{2,1,0:T(8,128)S(1)} collective-permute-done((f32[6,64,128]{2,1,0:T(8,128)S(1)}, f32[6,64,128]{2,1,0:T(8,128)S(1)}, u32[]{:S(2)}, u32[]{:S(2)}) %collective-permute-start.11) | collective-permute-done | bytes 196640 | tf_op jit(solution)/shard_map/ppermute | solution.py:473
  122.9 12.3 %grid_steps.7 = (f32[6,288,128]{2,1,0:T(8,128)S(1)}, f32[3,256,128]{2,1,0:T(8,128)S(1)}) custom-call(s32[4]{0:T(128)S(1)} %add_convert_fusion.edge, bf16[256,256]{1,0:T(8,128)(2,1)S(1)} %copy-done.1, f32[6,256,128]{2,1,0:T(8,128)S(1)} %get-tuple-element.26.refs_0_, f32[6,64,128]{2,1,0:T(8,128)S(1)} %constant_dynamic-update-slice_fusion.2.refs_1_, ...), custom_call_target="tpu_custom_call" | custom-call | flops 40000000 | bytes 8388608 | tf_op jit(solution)/shard_map/grid_steps/pallas_call | solution.py:295
  135.2 0.1 collective-permute-start.14
  135.3 5.1 %collective-permute-start.15 = (f32[6,288,128]{2,1,0:T(8,128)S(1)}, f32[6,288,128]{2,1,0:T(8,128)S(1)}, u32[]{:S(2)}, u32[]{:S(2)}) collective-permute-start(f32[6,288,128]{2,1,0:T(8,128)S(1)} %get-tuple-element.29.refs_0_), channel_id=1, source_target_pairs={{0,124},{4,0},{8,4},{12,8},{16,12},{20,16},{24,20},{28,24},{32,28}... | collective-permute-start | bytes 2654216 | tf_op jit(solution)/shard_map/ppermute | solution.py:473
  140.3 10.7 %collective-permute-done.14.refs_1_ = f32[6,288,128]{2,1,0:T(8,128)S(1)} collective-permute-done((f32[6,288,128]{2,1,0:T(8,128)S(1)}, f32[6,288,128]{2,1,0:T(8,128)S(1)}, u32[]{:S(2)}, u32[]{:S(2)}) %collective-permute-start.14) | collective-permute-done | bytes 884768 | tf_op jit(solution)/shard_map/ppermute | solution.py:473
  151.1 10.0 %grid_steps.8 = (f32[6,256,128]{2,1,0:T(8,128)S(1)}, f32[6,16,128]{2,1,0:T(8,128)S(1)}, f32[6,16,128]{2,1,0:T(8,128)S(1)}, f32[3,256,128]{2,1,0:T(8,128)S(1)}) custom-call(s32[4]{0:T(128)S(1)} %add_convert_fusion.edge, bf16[256,256]{1,0:T(8,128)(2,1)S(1)} %copy-done.1, f32[6,288,128]{2,1,0:T(8,128)S(1)} %get-tuple-element.29.refs_0_, ...), custom_call_target="tpu_custom_call" | custom-call | flops 40000000 | bytes 8388608 | tf_op jit(solution)/shard_map/grid_steps/pallas_call | solution.py:295
  161.0 0.7 copy-done.5
  161.8 5.1 %collective-permute-start.20 = (f32[6,256,128]{2,1,0:T(8,128)S(1)}, f32[6,256,128]{2,1,0:T(8,128)}, u32[]{:S(2)}, u32[]{:S(2)}) collective-permute-start(f32[6,256,128]{2,1,0:T(8,128)S(1)} %get-tuple-element.30.refs_0_), channel_id=1, source_target_pairs={{0,124},{4,0},{8,4},{12,8},{16,12},{20,16},{24,20},{28,24},{32,28}... | collective-permute-start | bytes 2359304 | tf_op jit(solution)/shard_map/ppermute | solution.py:473
  166.9 2.4 %slice.9 = f32[3,8,32,4]{3,2,1,0:T(8,128)} slice(f32[3,8,32,128]{3,2,1,0:T(8,128)S(1)} %bitcast.22), slice={[0:3:1], [0:8:1], [0:32:1], [0:128:32]} | slice | bytes 24576 | tf_op jit(solution)/shard_map/slice | solution.py:514
  169.2 1.2 copy.19
  170.4 0.1 reshape.43
  170.6 2.4 %slice.10 = f32[3,8,32,4]{3,2,1,0:T(8,128)} slice(f32[3,8,32,128]{3,2,1,0:T(8,128)S(1)} %bitcast.23), slice={[0:3:1], [0:8:1], [0:32:1], [0:128:32]} | slice | bytes 24576 | tf_op jit(solution)/shard_map/slice | solution.py:514
  173.0 1.3 copy.20
  174.3 0.1 reshape.45
  174.4 1.2 collective-permute-start.16
  175.6 0.9 collective-permute-start.17
  176.5 4.2 %slice.11 = f32[3,8,32,4]{3,2,1,0:T(8,128)} slice(f32[3,8,32,128]{3,2,1,0:T(8,128)} %bitcast.24), slice={[0:3:1], [0:8:1], [0:32:1], [0:128:32]} | slice | bytes 24576 | tf_op jit(solution)/shard_map/slice | solution.py:514
  180.7 1.2 copy.21
  181.9 0.1 reshape.47
  182.0 0.0 collective-permute-done.16
  182.0 0.1 collective-permute-start.19
  182.1 5.1 %collective-permute-start.21 = (f32[6,32,128]{2,1,0:T(8,128)S(1)}, f32[6,32,128]{2,1,0:T(8,128)S(1)}, u32[]{:S(2)}, u32[]{:S(2)}) collective-permute-start(f32[6,32,128]{2,1,0:T(8,128)S(1)} %constant_dynamic-update-slice_fusion.4.refs_1_), channel_id=1, source_target_pairs={{0,124},{4,0},{8,4},{12,8},{16,12},{20,16},{24,20},{28,24},{32,28}... | collective-permute-start | bytes 294920 | tf_op jit(solution)/shard_map/ppermute | solution.py:473
  187.1 2.3 collective-permute-done.19.refs_3_
  189.5 11.3 %grid_steps.9 = (f32[768,128]{1,0:T(8,128)}, f32[24,128]{1,0:T(8,128)S(1)}) custom-call(s32[4]{0:T(128)S(1)} %add_convert_fusion.edge, bf16[256,256]{1,0:T(8,128)(2,1)S(1)} %copy-done.1, f32[6,256,128]{2,1,0:T(8,128)S(1)} %get-tuple-element.30.refs_0_, f32[6,32,128]{2,1,0:T(8,128)S(1)} %constant_dynamic-update-slice_fusion.4.refs_1_, ...), custom_call_target="tpu_custom_call" | custom-call | flops 40000000 | bytes 8388608 | tf_op jit(solution)/shard_map/grid_steps/pallas_call | solution.py:295
  200.8 0.5 collective-permute-start.24
  201.3 2.7 %collective-permute-start.23 = (f32[96,128]{1,0:T(8,128)S(1)}, f32[96,128]{1,0:T(8,128)S(1)}, u32[]{:S(2)}, u32[]{:S(2)}) collective-permute-start(f32[96,128]{1,0:T(8,128)S(1)} %constant_dynamic-update-slice_fusion.6), channel_id=1, source_target_pairs={{0,2},{1,3},{2,0},{3,1},{4,6},{5,7},{6,4},{7,5},{8,10},{9,11},{10,... | collective-permute-start | bytes 147464 | tf_op jit(solution)/shard_map/ppermute | solution.py:473
  204.0 1.0 collective-permute-start.22
  205.1 1.8 collective-permute-done.23
  206.9 1.2 collective-permute-done.22
  208.1 0.0 all-gather.2.cloned.1.call-done.table
  208.2 13.9 %buildings.1 = f32[1024,256]{1,0:T(8,128)} custom-call(s32[1024]{0:T(1024)S(1)} %bitcast.31, s32[1,1024]{1,0:T(1,128)S(1)} %bitcast.30, s32[1,1024]{1,0:T(1,128)S(1)} %bitcast.29, f32[4,96,128]{2,1,0:T(8,128)S(1)} %pad_maximum_fusion.surface, f32[1024,4,8,128]{3,2,1,0:T(8,128)} %all-gather.2.cloned.1.call-done.table), custom_call_target="tpu_custom_call" | custom-call | flops 20000000 | bytes 18874368 | tf_op jit(solution)/shard_map/buildings/pallas_call | solution.py:457
  (44 shorter events, 0.2 us)
Async XLA Ops:
  7.2 201.0 %all-gather.2.cloned.1.call-start = ((), (), s32[]{:S(2)}) async-start(), calls=%async_computation | async-start | bytes 16908288 | tf_op jit(solution)/shard_map/all_gather | solution.py:495
  8.0 1.2 copy-start.2
  9.2 10.4 %copy-start.6 = (f32[3,32,8,128]{3,2,1,0:T(8,128)S(1)}, f32[3,32,8,128]{3,2,1,0:T(8,128)}, u32[]{:S(2)}) copy-start(f32[3,32,8,128]{3,2,1,0:T(8,128)} %param.9) | copy-start | bytes 1179652
  9.2 10.4 %copy-start.7 = (f32[3,32,8,128]{3,2,1,0:T(8,128)S(1)}, f32[3,32,8,128]{3,2,1,0:T(8,128)}, u32[]{:S(2)}) copy-start(f32[3,32,8,128]{3,2,1,0:T(8,128)} %param.10) | copy-start | bytes 1179652
  9.2 10.4 %copy-start.8 = (f32[32,8,128]{2,1,0:T(8,128)S(1)}, f32[32,8,128]{2,1,0:T(8,128)}, u32[]{:S(2)}) copy-start(f32[32,8,128]{2,1,0:T(8,128)} %param.11) | copy-start | bytes 393220
  9.2 10.4 %copy-start.9 = (f32[32,8,128]{2,1,0:T(8,128)S(1)}, f32[32,8,128]{2,1,0:T(8,128)}, u32[]{:S(2)}) copy-start(f32[32,8,128]{2,1,0:T(8,128)} %param.12) | copy-start | bytes 393220
  19.5 25.0 %copy-start.1 = (bf16[256,256]{1,0:T(8,128)(2,1)S(1)}, bf16[256,256]{1,0:T(8,128)(2,1)}, u32[]{:S(2)}) copy-start(bf16[256,256]{1,0:T(8,128)(2,1)} %constant.77.clone.weights_ref) | copy-start | bytes 393220
  20.8 22.7 %collective-permute-start.2 = (f32[8,256,128]{2,1,0:T(8,128)S(1)}, f32[8,256,128]{2,1,0:T(8,128)S(1)}, u32[]{:S(2)}, u32[]{:S(2)}) collective-permute-start(f32[8,256,128]{2,1,0:T(8,128)S(1)} %get-tuple-element.20.refs_0_), channel_id=1, source_target_pairs={{0,4},{4,8},{8,12},{12,16},{16,20},{20,24},{24,28},{28,32},{32,36}... | collective-permute-start | bytes 3145736 | tf_op jit(solution)/shard_map/ppermute | solution.py:473
  20.9 22.7 %collective-permute-start.4 = (f32[8,256,128]{2,1,0:T(8,128)S(1)}, f32[8,256,128]{2,1,0:T(8,128)S(1)}, u32[]{:S(2)}, u32[]{:S(2)}) collective-permute-start(f32[8,256,128]{2,1,0:T(8,128)S(1)} %get-tuple-element.20.refs_0_), channel_id=1, source_target_pairs={{0,124},{4,0},{8,4},{12,8},{16,12},{20,16},{24,20},{28,24},{32,28}... | collective-permute-start | bytes 3145736 | tf_op jit(solution)/shard_map/ppermute | solution.py:473
  26.6 5.0 %collective-permute-start = (f32[8,32,128]{2,1,0:T(8,128)S(1)}, f32[8,32,128]{2,1,0:T(8,128)S(1)}, u32[]{:S(2)}, u32[]{:S(2)}) collective-permute-start(f32[8,32,128]{2,1,0:T(8,128)S(1)} %get-tuple-element.21), channel_id=1, source_target_pairs={{0,1},{1,2},{2,3},{3,0},{4,5},{5,6},{6,7},{7,4},{8,9},{9,10},{10,1... | collective-permute-start | bytes 393224 | tf_op jit(solution)/shard_map/ppermute | solution.py:473
  27.9 5.0 %collective-permute-start.1 = (f32[8,32,128]{2,1,0:T(8,128)S(1)}, f32[8,32,128]{2,1,0:T(8,128)S(1)}, u32[]{:S(2)}, u32[]{:S(2)}) collective-permute-start(f32[8,32,128]{2,1,0:T(8,128)S(1)} %get-tuple-element.22), channel_id=1, source_target_pairs={{0,3},{1,0},{2,1},{3,2},{4,7},{5,4},{6,5},{7,6},{8,11},{9,8},{10,9... | collective-permute-start | bytes 393224 | tf_op jit(solution)/shard_map/ppermute | solution.py:473
  33.5 10.0 %collective-permute-start.3 = (f32[8,64,128]{2,1,0:T(8,128)}, f32[8,64,128]{2,1,0:T(8,128)}, u32[]{:S(2)}, u32[]{:S(2)}) collective-permute-start(f32[8,64,128]{2,1,0:T(8,128)} %constant_dynamic-update-slice_fusion.refs_1_), channel_id=1, source_target_pairs={{0,4},{4,8},{8,12},{12,16},{16,20},{20,24},{24,28},{28,32},{32,36}... | collective-permute-start | bytes 786440 | tf_op jit(solution)/shard_map/ppermute | solution.py:473
  33.5 10.0 %collective-permute-start.5 = (f32[8,64,128]{2,1,0:T(8,128)}, f32[8,64,128]{2,1,0:T(8,128)}, u32[]{:S(2)}, u32[]{:S(2)}) collective-permute-start(f32[8,64,128]{2,1,0:T(8,128)} %constant_dynamic-update-slice_fusion.refs_1_), channel_id=1, source_target_pairs={{0,124},{4,0},{8,4},{12,8},{16,12},{20,16},{24,20},{28,24},{32,28}... | collective-permute-start | bytes 786440 | tf_op jit(solution)/shard_map/ppermute | solution.py:473
  43.5 1.0 copy-start.3
  44.5 1.2 copy-start.4
  59.0 17.9 %collective-permute-start.6 = (f32[6,288,128]{2,1,0:T(8,128)S(1)}, f32[6,288,128]{2,1,0:T(8,128)S(1)}, u32[]{:S(2)}, u32[]{:S(2)}) collective-permute-start(f32[6,288,128]{2,1,0:T(8,128)S(1)} %get-tuple-element.23.refs_0_), channel_id=1, source_target_pairs={{0,4},{4,8},{8,12},{12,16},{16,20},{20,24},{24,28},{28,32},{32,36}... | collective-permute-start | bytes 2654216 | tf_op jit(solution)/shard_map/ppermute | solution.py:473
  59.0 17.9 %collective-permute-start.7 = (f32[6,288,128]{2,1,0:T(8,128)S(1)}, f32[6,288,128]{2,1,0:T(8,128)S(1)}, u32[]{:S(2)}, u32[]{:S(2)}) collective-permute-start(f32[6,288,128]{2,1,0:T(8,128)S(1)} %get-tuple-element.23.refs_0_), channel_id=1, source_target_pairs={{0,124},{4,0},{8,4},{12,8},{16,12},{20,16},{24,20},{28,24},{32,28}... | collective-permute-start | bytes 2654216 | tf_op jit(solution)/shard_map/ppermute | solution.py:473
  87.0 35.9 %collective-permute-start.10 = (f32[6,256,128]{2,1,0:T(8,128)S(1)}, f32[6,256,128]{2,1,0:T(8,128)S(1)}, u32[]{:S(2)}, u32[]{:S(2)}) collective-permute-start(f32[6,256,128]{2,1,0:T(8,128)S(1)} %get-tuple-element.26.refs_0_), channel_id=1, source_target_pairs={{0,4},{4,8},{8,12},{12,16},{16,20},{20,24},{24,28},{28,32},{32,36}... | collective-permute-start | bytes 2359304 | tf_op jit(solution)/shard_map/ppermute | solution.py:473
  87.1 35.9 %collective-permute-start.12 = (f32[6,256,128]{2,1,0:T(8,128)S(1)}, f32[6,256,128]{2,1,0:T(8,128)S(1)}, u32[]{:S(2)}, u32[]{:S(2)}) collective-permute-start(f32[6,256,128]{2,1,0:T(8,128)S(1)} %get-tuple-element.26.refs_0_), channel_id=1, source_target_pairs={{0,124},{4,0},{8,4},{12,8},{16,12},{20,16},{24,20},{28,24},{32,28}... | collective-permute-start | bytes 2359304 | tf_op jit(solution)/shard_map/ppermute | solution.py:473
  92.1 6.7 %collective-permute-start.8 = (f32[6,32,128]{2,1,0:T(8,128)S(1)}, f32[6,32,128]{2,1,0:T(8,128)S(1)}, u32[]{:S(2)}, u32[]{:S(2)}) collective-permute-start(f32[6,32,128]{2,1,0:T(8,128)S(1)} %get-tuple-element.27), channel_id=1, source_target_pairs={{0,1},{1,2},{2,3},{3,0},{4,5},{5,6},{6,7},{7,4},{8,9},{9,10},{10,1... | collective-permute-start | bytes 294920 | tf_op jit(solution)/shard_map/ppermute | solution.py:473
  93.3 6.7 %collective-permute-start.9 = (f32[6,32,128]{2,1,0:T(8,128)S(1)}, f32[6,32,128]{2,1,0:T(8,128)S(1)}, u32[]{:S(2)}, u32[]{:S(2)}) collective-permute-start(f32[6,32,128]{2,1,0:T(8,128)S(1)} %get-tuple-element.28), channel_id=1, source_target_pairs={{0,3},{1,0},{2,1},{3,2},{4,7},{5,4},{6,5},{7,6},{8,11},{9,8},{10,9... | collective-permute-start | bytes 294920 | tf_op jit(solution)/shard_map/ppermute | solution.py:473
  100.0 22.9 %collective-permute-start.11 = (f32[6,64,128]{2,1,0:T(8,128)S(1)}, f32[6,64,128]{2,1,0:T(8,128)S(1)}, u32[]{:S(2)}, u32[]{:S(2)}) collective-permute-start(f32[6,64,128]{2,1,0:T(8,128)S(1)} %constant_dynamic-update-slice_fusion.2.refs_1_), channel_id=1, source_target_pairs={{0,4},{4,8},{8,12},{12,16},{16,20},{20,24},{24,28},{28,32},{32,36}... | collective-permute-start | bytes 589832 | tf_op jit(solution)/shard_map/ppermute | solution.py:473
  100.1 22.8 %collective-permute-start.13 = (f32[6,64,128]{2,1,0:T(8,128)S(1)}, f32[6,64,128]{2,1,0:T(8,128)S(1)}, u32[]{:S(2)}, u32[]{:S(2)}) collective-permute-start(f32[6,64,128]{2,1,0:T(8,128)S(1)} %constant_dynamic-update-slice_fusion.2.refs_1_), channel_id=1, source_target_pairs={{0,124},{4,0},{8,4},{12,8},{16,12},{20,16},{24,20},{28,24},{32,28}... | collective-permute-start | bytes 589832 | tf_op jit(solution)/shard_map/ppermute | solution.py:473
  135.2 15.9 %collective-permute-start.14 = (f32[6,288,128]{2,1,0:T(8,128)S(1)}, f32[6,288,128]{2,1,0:T(8,128)S(1)}, u32[]{:S(2)}, u32[]{:S(2)}) collective-permute-start(f32[6,288,128]{2,1,0:T(8,128)S(1)} %get-tuple-element.29.refs_0_), channel_id=1, source_target_pairs={{0,4},{4,8},{8,12},{12,16},{16,20},{20,24},{24,28},{28,32},{32,36}... | collective-permute-start | bytes 2654216 | tf_op jit(solution)/shard_map/ppermute | solution.py:473
  135.3 15.8 %collective-permute-start.15 = (f32[6,288,128]{2,1,0:T(8,128)S(1)}, f32[6,288,128]{2,1,0:T(8,128)S(1)}, u32[]{:S(2)}, u32[]{:S(2)}) collective-permute-start(f32[6,288,128]{2,1,0:T(8,128)S(1)} %get-tuple-element.29.refs_0_), channel_id=1, source_target_pairs={{0,124},{4,0},{8,4},{12,8},{16,12},{20,16},{24,20},{28,24},{32,28}... | collective-permute-start | bytes 2654216 | tf_op jit(solution)/shard_map/ppermute | solution.py:473
  161.0 0.7 copy-start.5
  161.8 27.7 %collective-permute-start.18 = (f32[6,256,128]{2,1,0:T(8,128)S(1)}, f32[6,256,128]{2,1,0:T(8,128)}, u32[]{:S(2)}, u32[]{:S(2)}) collective-permute-start(f32[6,256,128]{2,1,0:T(8,128)S(1)} %get-tuple-element.30.refs_0_), channel_id=1, source_target_pairs={{0,4},{4,8},{8,12},{12,16},{16,20},{20,24},{24,28},{28,32},{32,36}... | collective-permute-start | bytes 2359304 | tf_op jit(solution)/shard_map/ppermute | solution.py:473
  161.8 27.7 %collective-permute-start.20 = (f32[6,256,128]{2,1,0:T(8,128)S(1)}, f32[6,256,128]{2,1,0:T(8,128)}, u32[]{:S(2)}, u32[]{:S(2)}) collective-permute-start(f32[6,256,128]{2,1,0:T(8,128)S(1)} %get-tuple-element.30.refs_0_), channel_id=1, source_target_pairs={{0,124},{4,0},{8,4},{12,8},{16,12},{20,16},{24,20},{28,24},{32,28}... | collective-permute-start | bytes 2359304 | tf_op jit(solution)/shard_map/ppermute | solution.py:473
  173.0 16.5 %copy-start = (f32[28,80,128]{2,1,0:T(8,128)S(1)}, f32[28,80,128]{2,1,0:T(8,128)}, u32[]{:S(2)}) copy-start(f32[28,80,128]{2,1,0:T(8,128)} %get-tuple-element.25.refs_4_.refs_7_) | copy-start | bytes 3440644
  174.4 7.6 %collective-permute-start.16 = (f32[6,16,128]{2,1,0:T(8,128)S(1)}, f32[6,16,128]{2,1,0:T(8,128)S(1)}, u32[]{:S(2)}, u32[]{:S(2)}) collective-permute-start(f32[6,16,128]{2,1,0:T(8,128)S(1)} %get-tuple-element.31), channel_id=1, source_target_pairs={{0,1},{1,2},{2,3},{3,0},{4,5},{5,6},{6,7},{7,4},{8,9},{9,10},{10,1... | collective-permute-start | bytes 147464 | tf_op jit(solution)/shard_map/ppermute | solution.py:473
  175.6 6.4 %collective-permute-start.17 = (f32[6,16,128]{2,1,0:T(8,128)S(1)}, f32[6,16,128]{2,1,0:T(8,128)S(1)}, u32[]{:S(2)}, u32[]{:S(2)}) collective-permute-start(f32[6,16,128]{2,1,0:T(8,128)S(1)} %get-tuple-element.32), channel_id=1, source_target_pairs={{0,3},{1,0},{2,1},{3,2},{4,7},{5,4},{6,5},{7,6},{8,11},{9,8},{10,9... | collective-permute-start | bytes 147464 | tf_op jit(solution)/shard_map/ppermute | solution.py:473
  182.0 7.4 %collective-permute-start.19 = (f32[6,32,128]{2,1,0:T(8,128)S(1)}, f32[6,32,128]{2,1,0:T(8,128)S(1)}, u32[]{:S(2)}, u32[]{:S(2)}) collective-permute-start(f32[6,32,128]{2,1,0:T(8,128)S(1)} %constant_dynamic-update-slice_fusion.4.refs_1_), channel_id=1, source_target_pairs={{0,4},{4,8},{8,12},{12,16},{16,20},{20,24},{24,28},{28,32},{32,36}... | collective-permute-start | bytes 294920 | tf_op jit(solution)/shard_map/ppermute | solution.py:473
  182.1 7.4 %collective-permute-start.21 = (f32[6,32,128]{2,1,0:T(8,128)S(1)}, f32[6,32,128]{2,1,0:T(8,128)S(1)}, u32[]{:S(2)}, u32[]{:S(2)}) collective-permute-start(f32[6,32,128]{2,1,0:T(8,128)S(1)} %constant_dynamic-update-slice_fusion.4.refs_1_), channel_id=1, source_target_pairs={{0,124},{4,0},{8,4},{12,8},{16,12},{20,16},{24,20},{28,24},{32,28}... | collective-permute-start | bytes 294920 | tf_op jit(solution)/shard_map/ppermute | solution.py:473
  187.1 17.9 %copy-start.11 = (s32[1024]{0:T(1024)S(1)}, s32[1024]{0:T(1024)}, u32[]{:S(2)}) copy-start(s32[1024]{0:T(1024)} %param.13) | copy-start | bytes 12292
  187.1 21.0 %copy-start.10 = (s32[1024,1]{0,1:T(1,128)S(1)}, s32[1024,1]{0,1:T(1,128)}, u32[]{:S(2)}) copy-start(s32[1024,1]{0,1:T(1,128)} %param.14) | copy-start | bytes 12292
  200.8 4.3 %collective-permute-start.24 = (f32[96,128]{1,0:T(8,128)S(1)}, f32[96,128]{1,0:T(8,128)S(1)}, u32[]{:S(2)}, u32[]{:S(2)}) collective-permute-start(f32[96,128]{1,0:T(8,128)S(1)} %constant_dynamic-update-slice_fusion.6), channel_id=1, source_target_pairs={{0,3},{1,0},{2,1},{3,2},{4,7},{5,4},{6,5},{7,6},{8,11},{9,8},{10,9... | collective-permute-start | bytes 147464 | tf_op jit(solution)/shard_map/ppermute | solution.py:473
  201.3 5.6 %collective-permute-start.23 = (f32[96,128]{1,0:T(8,128)S(1)}, f32[96,128]{1,0:T(8,128)S(1)}, u32[]{:S(2)}, u32[]{:S(2)}) collective-permute-start(f32[96,128]{1,0:T(8,128)S(1)} %constant_dynamic-update-slice_fusion.6), channel_id=1, source_target_pairs={{0,2},{1,3},{2,0},{3,1},{4,6},{5,7},{6,4},{7,5},{8,10},{9,11},{10,... | collective-permute-start | bytes 147464 | tf_op jit(solution)/shard_map/ppermute | solution.py:473
  204.0 4.1 %collective-permute-start.22 = (f32[96,128]{1,0:T(8,128)S(1)}, f32[96,128]{1,0:T(8,128)S(1)}, u32[]{:S(2)}, u32[]{:S(2)}) collective-permute-start(f32[96,128]{1,0:T(8,128)S(1)} %constant_dynamic-update-slice_fusion.6), channel_id=1, source_target_pairs={{0,1},{1,2},{2,3},{3,0},{4,5},{5,6},{6,7},{7,4},{8,9},{9,10},{10,1... | collective-permute-start | bytes 147464 | tf_op jit(solution)/shard_map/ppermute | solution.py:473
Sparse Core Ops, SparseCore 0:
  19.7 101.7 all-gather.1

commit v2 on v1

--- a/solution.py
+++ b/solution.py
@@ -23,8 +23,10 @@
 R0 = 8 * max(TILES_Y) + 8
 RE = 2 * R0 + ROWS
 CHUNK = 4
+SCALES = (2.0**64, 2.0**32, 1.0, 1.0)
 VMEM = pl.BlockSpec(memory_space=pltpu.VMEM)
 SMEM = pl.BlockSpec(memory_space=pltpu.SMEM)
+HBM = pl.BlockSpec(memory_space=pltpu.HBM)
 
 
 def depth_weights():
@@ -200,6 +202,21 @@
     lax.fori_loop(0, CX // 4, columns, 0)
 
 
+def surface_of(field, snap):
+    count = 3 * CX
+    depth = lax.broadcasted_iota(jnp.int32, (ROWS, 128), 1) % NZ
+    gathered = field[0, X0, pl.ds(R0, ROWS), :]
+    for k in range(1, count):
+        layer = pltpu.roll(field[k // CX, X0 + k % CX, pl.ds(R0, ROWS), :], k, 1)
+        gathered = jnp.where(depth == k, layer, gathered)
+    across = jnp.concatenate([gathered] * GROUPS).T
+    lanes = block_of_lanes((count, CY))
+    result = across[0:count]
+    for g in range(1, GROUPS):
+        result = jnp.where(lanes == g, across[NZ * g : NZ * g + count], result)
+    snap[...] = result
+
+
 def grid_kernel(block, merged, snap_step, edge, weights_ref, *refs):
     first, last = block == 0, block == len(TILES_Y) - 1
     tiles_y = TILES_Y[block]
@@ -211,6 +228,8 @@
         shear, bulk = take(2)
     else:
         shear, bulk = take(2)
+        if last:
+            take(1)
         sends = take(1) if last or TILES_Y[block + 1] < tiles_y else take(3)
     snap = take(1)[0] if snap_step is not None else None
     fields = take(2)
@@ -240,8 +259,7 @@
         advance(step, tiles_y, now, before, shear, bulk, refs, weights_ref)
         now, before = before, now
         if step == snap_step and not last:
-            for x in range(CX):
-                snap[:, pl.ds(ROWS * x, ROWS), :] = now[:, X0 + x, pl.ds(R0, ROWS), :]
+            surface_of(now, snap)
     if last:
         whole = sends[0]
         for c in range(3):
@@ -273,7 +291,7 @@
                 out[f, pl.ds(start + 8 * depth * q, 8 * depth), :] = pick_block(columns, group)
 
 
-def run_grid(block, snap_step, edge, weights, blocks, coefs):
+def run_grid(block, snap_step, edge, weights, blocks, coefs, after=None):
     shape = lambda *s: jax.ShapeDtypeStruct(s, jnp.float32)
     last = block == len(TILES_Y) - 1
     merged = len(blocks[0]) == 1
@@ -288,14 +306,18 @@
         outs += [shape(XE, RE, 128)] * 2
     else:
         operands += list(coefs)
+    specs = [SMEM] + [VMEM] * (len(operands) - 1)
+    if last:
+        operands.append(after)
+        specs.append(HBM)
     if snap_step is not None:
-        outs.append(shape(3 * CX, CY) if last else shape(3, CX * ROWS, 128))
+        outs.append(shape(3 * CX, CY))
     field = pltpu.VMEM((3, XE, RE, 128), jnp.float32)
     plane = pltpu.VMEM((XE, RE, 128), jnp.float32)
     return pl.pallas_call(
         functools.partial(grid_kernel, block, merged, snap_step),
         out_shape=outs,
-        in_specs=[SMEM] + [VMEM] * (len(operands) - 1),
+        in_specs=specs,
         out_specs=[VMEM] * len(outs),
         scratch_shapes=[field, field, field, plane, plane, plane, plane],
         compiler_params=pltpu.CompilerParams(vmem_limit_bytes=48 << 20),
@@ -341,10 +363,11 @@
     )(*flat)
 
 
-def response_kernel(transition, forcing, out, state, total):
+def response_kernel(transition, forcing, out, state, total, flipped):
     arch = transition.shape[0]
+    for a in range(arch):
+        flipped[a] = transition[a].T
     state[...] = jnp.zeros_like(state)
-    out[...] = jnp.zeros_like(out)
     for a in range(arch):
         state[a, 0:3, :] = forcing[a]
 
@@ -356,8 +379,8 @@
             low = (now - high.astype(jnp.float32)).astype(jnp.bfloat16)
             product = lax.dot_general(
                 jnp.concatenate([high, low], axis=0),
-                transition[a],
-                (((1,), (1,)), ((), ())),
+                flipped[a],
+                (((1,), (0,)), ((), ())),
                 preferred_element_type=jnp.float32,
             )
             state[a] = product[0:8] + product[8:16]
@@ -366,28 +389,25 @@
     for group in range(COUPLINGS):
         moment = COUPLINGS - 1 - group
         total[...] = jnp.zeros_like(total)
-        lax.fori_loop(0, SUB, one, 0)
+        lax.fori_loop(0, SUB, one, 0, unroll=True)
         for a in range(arch):
             for c in range(3):
                 for h in range(2):
-                    row = 2 * c + h
-                    out[a, moment, row : row + 1, :] = total[
-                        a, c : c + 1, 128 * h : 128 * h + 128
-                    ]
-            if group < COUPLINGS - 1:
-                scale = jnp.maximum(jnp.max(jnp.abs(state[a]), keepdims=True), 1.0)
-                state[a] = state[a] / scale
-                out[a, moment, 6:7, :] = jnp.broadcast_to(scale, (1, 128))
+                    row = 6 * moment + 2 * c + h
+                    out[a, row : row + 1, :] = total[a, c : c + 1, 128 * h : 128 * h + 128]
+            if SCALES[moment - 1] != SCALES[moment]:
+                state[a] = state[a] * (SCALES[moment] / SCALES[moment - 1])
 
 
 def responses(transition, forcing):
     arch, width = transition.shape[0], transition.shape[1]
     return pl.pallas_call(
         response_kernel,
-        out_shape=jax.ShapeDtypeStruct((arch, COUPLINGS, 8, 128), jnp.float32),
+        out_shape=jax.ShapeDtypeStruct((arch, 6 * COUPLINGS, 128), jnp.float32),
         in_specs=[VMEM, VMEM],
         out_specs=VMEM,
-        scratch_shapes=[pltpu.VMEM((arch, 8, width), jnp.float32)] * 2,
+        scratch_shapes=[pltpu.VMEM((arch, 8, width), jnp.float32)] * 2
+        + [pltpu.VMEM((arch, width, width), jnp.bfloat16)],
         compiler_params=pltpu.CompilerParams(vmem_limit_bytes=24 << 20),
         cost_estimate=pl.CostEstimate(
             flops=20_000_000, bytes_accessed=2 << 20, transcendentals=0
@@ -396,7 +416,13 @@
     )(transition, forcing)
 
 
-def building_kernel(kinds, place, across, surface, table, out, ground):
+def building_kernel(tiles, kinds, place, across, surface, table_ref, *refs):
+    before = refs[0] if len(refs) == 5 else None
+    out, ground, table, arrived = refs[-4:]
+    fetch = pltpu.make_async_copy(
+        table_ref.at[:, pl.ds(8 * tiles[0], 8 * len(tiles)), :], table, arrived
+    )
+    fetch.start()
     count = out.shape[0]
     cells = surface.shape[0] * CY
     picks = (lax.broadcasted_iota(jnp.int32, (cells, count), 0) == place[...]).astype(jnp.bfloat16)
@@ -412,19 +438,21 @@
     picked = picked[0:n] + picked[n : 2 * n] + picked[2 * n : 3 * n]
     here = lax.broadcasted_iota(jnp.int32, (CX, count), 0) == across[...]
     row = lax.broadcasted_iota(jnp.int32, (8, count), 0)
-    for m in range(COUPLINGS):
+    first = 4 * tiles[0] // 3 * 3
+    for t, tile in enumerate(tiles):
         rows = []
-        for c in range(3):
-            k = 3 * m + c
-            value = jnp.where(here, picked[CX * k : CX * k + CX], 0.0)
-            rows.append(jnp.sum(value, axis=0, keepdims=True))
-        ground[m] = jnp.where(
-            row < 2, rows[0], jnp.where(row < 4, rows[1], jnp.where(row < 6, rows[2], 0.0))
+        for k in range(4 * tile, 4 * tile + 4):
+            at = CX * (k - first)
+            value = jnp.where(here, picked[at : at + CX], 0.0)
+            rows.append(jnp.sum(value, axis=0, keepdims=True) * SCALES[k // 3])
+        ground[t] = jnp.where(
+            row < 4, jnp.where(row < 2, rows[0], rows[1]), jnp.where(row < 6, rows[2], rows[3])
         )
-
-    def tile(t, carry):
+    fetch.wait()
+
+    def some(t, carry):
         base = pl.multiple_of(t * 128, 128)
-        motion = [ground[m, :, pl.ds(base, 128)] for m in range(COUPLINGS)]
+        motion = [ground[k, :, pl.ds(base, 128)] for k in range(len(tiles))]
         slot = lax.broadcasted_iota(jnp.int32, (8, 128), 0)
         for eight in range(16):
             halves = [jnp.zeros((8, 128), jnp.float32)] * 2
@@ -432,40 +460,44 @@
                 i = 8 * eight + k
                 kind = kinds[base + i]
                 total = None
-                for m in range(COUPLINGS):
-                    term = table[kind, m] * jnp.broadcast_to(motion[m][:, i : i + 1], (8, 128))
-                    if total is None:
-                        total = term
-                    else:
-                        scale = jnp.broadcast_to(table[kind, m, 6:7, :], (8, 128))
-                        total = total * scale + term
+                for j in range(len(tiles)):
+                    term = table[kind, 8 * j : 8 * j + 8, :] * jnp.broadcast_to(
+                        motion[j][:, i : i + 1], (8, 128)
+                    )
+                    total = term if total is None else total + term
                 total = total + pltpu.roll(total, 4, 0)
                 total = total + pltpu.roll(total, 2, 0)
                 other = pltpu.roll(total, 1, 0)
                 pair = (total, other) if k % 2 == 0 else (other, total)
                 halves = [jnp.where(slot == k, new, old) for new, old in zip(pair, halves)]
             rows = pl.ds(base + 8 * eight, 8)
-            out[rows, 0:128] = halves[0]
-            out[rows, 128:256] = halves[1]
+            for h in range(2):
+                lanes = slice(128 * h, 128 * h + 128)
+                out[rows, lanes] = halves[h] if before is None else halves[h] + before[rows, lanes]
         return carry
 
-    lax.fori_loop(0, count // 128, tile, 0)
-
-
-def building_states(kinds, place, across, surface, table, width):
+    lax.fori_loop(0, count // 128, some, 0)
+
+
+def building_states(tiles, kinds, place, across, surface, table, width, before=None):
     count = kinds.shape[0]
+    more = [] if before is None else [before]
     return pl.pallas_call(
-        building_kernel,
+        functools.partial(building_kernel, tiles),
         out_shape=jax.ShapeDtypeStruct((count, width), jnp.float32),
-        in_specs=[SMEM] + [VMEM] * 4,
+        in_specs=[SMEM] + [VMEM] * 3 + [HBM] + [VMEM] * len(more),
         out_specs=VMEM,
-        scratch_shapes=[pltpu.VMEM((COUPLINGS, 8, count), jnp.float32)],
-        compiler_params=pltpu.CompilerParams(vmem_limit_bytes=50 << 20),
+        scratch_shapes=[
+            pltpu.VMEM((len(tiles), 8, count), jnp.float32),
+            pltpu.VMEM((table.shape[0], 8 * len(tiles), 128), jnp.float32),
+            pltpu.SemaphoreType.DMA,
+        ],
+        compiler_params=pltpu.CompilerParams(vmem_limit_bytes=56 << 20),
         cost_estimate=pl.CostEstimate(
-            flops=20_000_000, bytes_accessed=18 << 20, transcendentals=0
+            flops=20_000_000, bytes_accessed=10 << 20, transcendentals=0
         ),
         name="buildings",
-    )(kinds, place[None, :], across[None, :], surface, table)
+    )(kinds, place[None, :], across[None, :], surface, table, *more)
 
 
 def ring(value, axis, shift):
@@ -494,33 +526,41 @@
     blocks = exchange(*arrange(displacement, previous, shear_coef, bulk_coef))
     table = lax.all_gather(responses(transition, forcing), ("slab", "gy"), axis=0, tiled=True)
 
+    columns = strips * CY
+    along_y = cell_index % columns
+    across = cell_index // columns - slab * CX
+    place = (gy - along_y // CY) % strips * CY + along_y % CY
+    kinds = archetype_id[:, 0]
+
+    def gathered(surface):
+        return jnp.stack(
+            [surface] + [ring(surface, "gy", shift) for shift in range(1, strips)]
+        )
+
     snaps = []
     coefs = None
+    states = None
     count = len(TILES_Y)
     for block in range(count):
         snap_step = next(
             (s for s in range(1, STEPS + 1) if (block * STEPS + s) % EVERY == 0), None
         )
-        result = run_grid(block, snap_step, edge, weights, blocks, coefs)
-        sends = 3 if block < count - 1 and TILES_Y[block + 1] >= TILES_Y[block] else 1
+        last = block == count - 1
+        if last:
+            early = gathered(jnp.concatenate(snaps))
+            states = building_states((0, 1), kinds, place, across, early, table, width)
+        result = run_grid(block, snap_step, edge, weights, blocks, coefs, states)
+        sends = 3 if not last and TILES_Y[block + 1] >= TILES_Y[block] else 1
         if block == 0:
             coefs = result[sends : sends + 2]
-        if block == count - 1:
-            final = result[0].reshape(3, NZ, CX, CY)
-            snaps.append(result[1])
-        else:
+        if not last:
             blocks = exchange(*result[:sends])
-            if snap_step is not None:
-                ground = result[-1].reshape(3, CX, ROWS, 128)[..., ::NZ]
-                snaps.append(ground.transpose(0, 1, 3, 2).reshape(3 * CX, CY))
-
-    mine = jnp.concatenate(snaps)
-    surface = jnp.stack([mine] + [ring(mine, "gy", shift) for shift in range(1, strips)])
-    columns = strips * CY
-    along_y = cell_index % columns
-    across = cell_index // columns - slab * CX
-    place = (gy - along_y // CY) % strips * CY + along_y % CY
-    states = building_states(archetype_id[:, 0], place, across, surface, table, width)
+        if snap_step is not None:
+            snaps.append(result[-1])
+    final = result[0].reshape(3, NZ, CX, CY)
+    late = gathered(snaps[-1])
+    recent = jnp.concatenate([early[:, 2 * 3 * CX :], late], axis=1)
+    states = building_states((2,), kinds, place, across, recent, table, width, states)
     return (final, states)
 
 

time: 231 us -> 216 us (0.935)
  local copies, waits for them, and re-layouts: 19.3 us -> 8.03 us
  waiting for transfers between devices: 60.8 us -> 53.7 us
  starting transfers between devices: 52.1 us -> 56.8 us
  Pallas kernels: 82.3 us -> 79.2 us
    slice x3 -> x2, local copies, waits for them, and re-layouts: 8.99 us -> 0.01 us  [per_device(): recent = jnp.concatenate([early[:, 2 * 3 * CX:], late], axis=1)]
    ppermute x25 -> x28, waiting for transfers between devices: 60.8 us -> 53.7 us  [ring(): lax.ppermute(value, axis, [(i, (i + shift) % count) for i in range(count)])]
    ppermute x25 -> x28, starting transfers between devices: 52 us -> 56.8 us  [ring(): lax.ppermute(value, axis, [(i, (i + shift) % count) for i in range(count)])]
    pallas_call x2 -> x3, Pallas kernels: 24.2 us -> 20.4 us  [the longest x2 16.2 us: building_states(): pl.pallas_call(functools.partial(building_kernel, tiles), out_shape=jax.S...]
    unnamed x34 -> x30, local copies, waits for them, and re-layouts: 9.32 us -> 7.35 us
  transfers between devices with their start and end apart: 26 -> 29, of which waited for: 11 -> 12; matrix products, arithmetic and copies ran while one was open for 6% -> 1% of each run, Pallas kernels for 25% -> 27%
where the time goes in v2:
time: 216 us; the launch traced here: 214 us
  Pallas kernels  79.2 us (37%)
  starting transfers between devices  56.8 us (26%)
  waiting for transfers between devices  53.7 us (25%)
  between operations  14.3 us (7%)
  local copies, waits for them, and re-layouts  8.03 us (4%)
    pallas_call x5, Pallas kernels, run_grid(): pl.pallas_call(functools.partial(grid_kernel, block, merged, snap_step),...  57.7 us
    ppermute x28, starting transfers between devices, ring(): lax.ppermute(value, axis, [(i, (i + shift) % count) for i in range(count)])  56.8 us
    ppermute x28, waiting for transfers between devices, ring(): lax.ppermute(value, axis, [(i, (i + shift) % count) for i in range(count)])  53.7 us
    pallas_call x2, Pallas kernels, building_states(): pl.pallas_call(functools.partial(building_kernel, tiles), out_shape=jax.S...  16.2 us
    unnamed x30, local copies, waits for them, and re-layouts  7.35 us
  transfers between devices with their start and end apart: 29, of which 12 were waited for; matrix products, arithmetic and copies ran while one was open for 1% of the time, Pallas kernels for 27%

profile of v2, /device:TPU:16, one launch (start us, length us, event | category | flops | bytes accessed | tf_op | source)
XLA Modules:
  0.0 214.1 jit_solution(12808783849893567461)
XLA Ops:
  7.2 0.0 all-gather.2.cloned.1.call-start
  7.2 0.8 copy.12.forcing
  8.0 0.0 copy-start.4
  8.0 1.2 copy-done.4
  9.2 4.1 %responses.1 = f32[8,24,128]{2,1,0:T(8,128)} custom-call(bf16[8,256,256]{2,1,0:T(8,128)(2,1)S(1)} %copy-done.4, f32[8,3,256]{2,1,0:T(4,128)S(1)} %copy.12.forcing), custom_call_target="tpu_custom_call" | custom-call | flops 20000000 | bytes 2097152 | tf_op jit(solution)/shard_map/responses/pallas_call | solution.py:404
  13.3 0.0 all-gather.2.cloned.1.call-update
  13.4 1.2 arrange.1
  14.6 0.1 collective-permute-start.2
  14.7 5.7 %collective-permute-start.4 = (f32[8,256,128]{2,1,0:T(8,128)S(1)}, f32[8,256,128]{2,1,0:T(8,128)S(1)}, u32[]{:S(2)}, u32[]{:S(2)}) collective-permute-start(f32[8,256,128]{2,1,0:T(8,128)S(1)} %get-tuple-element.20.refs_0_), channel_id=1, source_target_pairs={{0,124},{4,0},{8,4},{12,8},{16,12},{20,16},{24,20},{28,24},{32,28}... | collective-permute-start | bytes 3145736 | tf_op jit(solution)/shard_map/ppermute | solution.py:505
  20.4 1.3 collective-permute-start
  21.7 0.7 collective-permute-start.1
  22.4 2.9 %collective-permute-done = f32[8,32,128]{2,1,0:T(8,128)S(1)} collective-permute-done((f32[8,32,128]{2,1,0:T(8,128)S(1)}, f32[8,32,128]{2,1,0:T(8,128)S(1)}, u32[]{:S(2)}, u32[]{:S(2)}) %collective-permute-start) | collective-permute-done | bytes 131104 | tf_op jit(solution)/shard_map/ppermute | solution.py:505
  25.4 0.7 constant_dynamic-update-slice_fusion.1
  26.0 0.6 collective-permute-done.1
  26.7 0.7 constant_dynamic-update-slice_fusion.refs_1_
  27.3 0.0 collective-permute-start.3
  27.3 5.1 %collective-permute-start.5 = (f32[8,64,128]{2,1,0:T(8,128)}, f32[8,64,128]{2,1,0:T(8,128)}, u32[]{:S(2)}, u32[]{:S(2)}) collective-permute-start(f32[8,64,128]{2,1,0:T(8,128)} %constant_dynamic-update-slice_fusion.refs_1_), channel_id=1, source_target_pairs={{0,124},{4,0},{8,4},{12,8},{16,12},{20,16},{24,20},{28,24},{32,28}... | collective-permute-start | bytes 786440 | tf_op jit(solution)/shard_map/ppermute | solution.py:505
  32.4 0.1 add_convert_fusion.edge
  32.5 4.7 %collective-permute-done.3.refs_3_ = f32[8,64,128]{2,1,0:T(8,128)} collective-permute-done((f32[8,64,128]{2,1,0:T(8,128)}, f32[8,64,128]{2,1,0:T(8,128)}, u32[]{:S(2)}, u32[]{:S(2)}) %collective-permute-start.3) | collective-permute-done | bytes 262176 | tf_op jit(solution)/shard_map/ppermute | solution.py:505
  37.2 0.0 collective-permute-done.4.refs_4_
  37.2 0.0 copy-start.5
  37.2 1.0 copy-done.5
  38.1 1.2 copy-done.6
  39.4 13.3 %grid_steps.5 = (f32[6,288,128]{2,1,0:T(8,128)S(1)}, f32[28,80,128]{2,1,0:T(8,128)S(1)}, f32[28,80,128]{2,1,0:T(8,128)}) custom-call(s32[4]{0:T(128)S(1)} %add_convert_fusion.edge, bf16[256,256]{1,0:T(8,128)(2,1)S(1)} %copy-done.3, f32[8,256,128]{2,1,0:T(8,128)S(1)} %get-tuple-element.20.refs_0_, f32[8,64,128]{2,1,0:T(8,128)} %constant_dynamic-update-slice_fusion.refs_1_, ...), custom_call_target="tpu_custom_call" | custom-call | flops 40000000 | bytes 8388608 | tf_op jit(solution)/shard_map/grid_steps/pallas_call | solution.py:317
  52.7 5.1 %collective-permute-start.7 = (f32[6,288,128]{2,1,0:T(8,128)S(1)}, f32[6,288,128]{2,1,0:T(8,128)S(1)}, u32[]{:S(2)}, u32[]{:S(2)}) collective-permute-start(f32[6,288,128]{2,1,0:T(8,128)S(1)} %get-tuple-element.23.refs_0_), channel_id=1, source_target_pairs={{0,124},{4,0},{8,4},{12,8},{16,12},{20,16},{24,20},{28,24},{32,28}... | collective-permute-start | bytes 2654216 | tf_op jit(solution)/shard_map/ppermute | solution.py:505
  57.7 12.1 %collective-permute-done.6.refs_1_ = f32[6,288,128]{2,1,0:T(8,128)S(1)} collective-permute-done((f32[6,288,128]{2,1,0:T(8,128)S(1)}, f32[6,288,128]{2,1,0:T(8,128)S(1)}, u32[]{:S(2)}, u32[]{:S(2)}) %collective-permute-start.6) | collective-permute-done | bytes 884768 | tf_op jit(solution)/shard_map/ppermute | solution.py:505
  69.9 1.3 copy-done
  71.1 9.6 %grid_steps.6 = (f32[6,256,128]{2,1,0:T(8,128)S(1)}, f32[6,32,128]{2,1,0:T(8,128)S(1)}, f32[6,32,128]{2,1,0:T(8,128)S(1)}, f32[24,128]{1,0:T(8,128)S(1)}) custom-call(s32[4]{0:T(128)S(1)} %add_convert_fusion.edge, bf16[256,256]{1,0:T(8,128)(2,1)S(1)} %copy-done.3, f32[6,288,128]{2,1,0:T(8,128)S(1)} %get-tuple-element.23.refs_0_, ...), custom_call_target="tpu_custom_call" | custom-call | flops 40000000 | bytes 8388608 | tf_op jit(solution)/shard_map/grid_steps/pallas_call | solution.py:317
  80.8 0.1 collective-permute-start.10
  80.8 5.1 %collective-permute-start.12 = (f32[6,256,128]{2,1,0:T(8,128)S(1)}, f32[6,256,128]{2,1,0:T(8,128)S(1)}, u32[]{:S(2)}, u32[]{:S(2)}) collective-permute-start(f32[6,256,128]{2,1,0:T(8,128)S(1)} %get-tuple-element.26.refs_0_), channel_id=1, source_target_pairs={{0,124},{4,0},{8,4},{12,8},{16,12},{20,16},{24,20},{28,24},{32,28}... | collective-permute-start | bytes 2359304 | tf_op jit(solution)/shard_map/ppermute | solution.py:505
  85.9 1.4 collective-permute-start.8
  87.3 0.6 collective-permute-start.9
  87.9 3.9 %collective-permute-done.8 = f32[6,32,128]{2,1,0:T(8,128)S(1)} collective-permute-done((f32[6,32,128]{2,1,0:T(8,128)S(1)}, f32[6,32,128]{2,1,0:T(8,128)S(1)}, u32[]{:S(2)}, u32[]{:S(2)}) %collective-permute-start.8) | collective-permute-done | bytes 98336 | tf_op jit(solution)/shard_map/ppermute | solution.py:505
  91.8 1.4 collective-permute-done.9
  93.3 0.1 collective-permute-start.11
  93.4 5.1 %collective-permute-start.13 = (f32[6,64,128]{2,1,0:T(8,128)S(1)}, f32[6,64,128]{2,1,0:T(8,128)S(1)}, u32[]{:S(2)}, u32[]{:S(2)}) collective-permute-start(f32[6,64,128]{2,1,0:T(8,128)S(1)} %constant_dynamic-update-slice_fusion.2.refs_1_), channel_id=1, source_target_pairs={{0,124},{4,0},{8,4},{12,8},{16,12},{20,16},{24,20},{28,24},{32,28}... | collective-permute-start | bytes 589832 | tf_op jit(solution)/shard_map/ppermute | solution.py:505
  98.4 11.6 %collective-permute-done.11.refs_3_ = f32[6,64,128]{2,1,0:T(8,128)S(1)} collective-permute-done((f32[6,64,128]{2,1,0:T(8,128)S(1)}, f32[6,64,128]{2,1,0:T(8,128)S(1)}, u32[]{:S(2)}, u32[]{:S(2)}) %collective-permute-start.11) | collective-permute-done | bytes 196640 | tf_op jit(solution)/shard_map/ppermute | solution.py:505
  110.0 12.4 %grid_steps.7 = (f32[6,288,128]{2,1,0:T(8,128)S(1)}, f32[24,128]{1,0:T(8,128)S(1)}) custom-call(s32[4]{0:T(128)S(1)} %add_convert_fusion.edge, bf16[256,256]{1,0:T(8,128)(2,1)S(1)} %copy-done.3, f32[6,256,128]{2,1,0:T(8,128)S(1)} %get-tuple-element.26.refs_0_, f32[6,64,128]{2,1,0:T(8,128)S(1)} %constant_dynamic-update-slice_fusion.2.refs_1_, ...), custom_call_target="tpu_custom_call" | custom-call | flops 40000000 | bytes 8388608 | tf_op jit(solution)/shard_map/grid_steps/pallas_call | solution.py:317
  122.4 0.1 collective-permute-start.14
  122.5 5.1 %collective-permute-start.15 = (f32[6,288,128]{2,1,0:T(8,128)S(1)}, f32[6,288,128]{2,1,0:T(8,128)}, u32[]{:S(2)}, u32[]{:S(2)}) collective-permute-start(f32[6,288,128]{2,1,0:T(8,128)S(1)} %get-tuple-element.29.refs_0_), channel_id=1, source_target_pairs={{0,124},{4,0},{8,4},{12,8},{16,12},{20,16},{24,20},{28,24},{32,28}... | collective-permute-start | bytes 2654216 | tf_op jit(solution)/shard_map/ppermute | solution.py:505
  127.5 10.8 %collective-permute-done.14.refs_1_ = f32[6,288,128]{2,1,0:T(8,128)} collective-permute-done((f32[6,288,128]{2,1,0:T(8,128)S(1)}, f32[6,288,128]{2,1,0:T(8,128)}, u32[]{:S(2)}, u32[]{:S(2)}) %collective-permute-start.14) | collective-permute-done | bytes 884768 | tf_op jit(solution)/shard_map/ppermute | solution.py:505
  138.4 11.2 %grid_steps.8 = (f32[6,256,128]{2,1,0:T(8,128)}, f32[6,16,128]{2,1,0:T(8,128)S(1)}, f32[6,16,128]{2,1,0:T(8,128)S(1)}, f32[24,128]{1,0:T(8,128)S(1)}) custom-call(s32[4]{0:T(128)S(1)} %add_convert_fusion.edge, bf16[256,256]{1,0:T(8,128)(2,1)S(1)} %copy-done.3, f32[6,288,128]{2,1,0:T(8,128)S(1)} %get-tuple-element.29.refs_0_, ...), custom_call_target="tpu_custom_call" | custom-call | flops 40000000 | bytes 8388608 | tf_op jit(solution)/shard_map/grid_steps/pallas_call | solution.py:317
  149.5 5.1 %collective-permute-start.20 = (f32[6,256,128]{2,1,0:T(8,128)}, f32[6,256,128]{2,1,0:T(8,128)}, u32[]{:S(2)}, u32[]{:S(2)}) collective-permute-start(f32[6,256,128]{2,1,0:T(8,128)} %get-tuple-element.30.refs_0_), channel_id=1, source_target_pairs={{0,124},{4,0},{8,4},{12,8},{16,12},{20,16},{24,20},{28,24},{32,28}... | collective-permute-start | bytes 2359304 | tf_op jit(solution)/shard_map/ppermute | solution.py:505
  154.6 0.6 fusion.4
  155.2 1.2 collective-permute-start.16
  156.4 0.5 collective-permute-start.22
  156.9 1.8 collective-permute-start.23
  158.7 0.6 collective-permute-done.16
  159.3 0.6 collective-permute-start.17
  159.9 3.5 %collective-permute-done.17 = f32[6,16,128]{2,1,0:T(8,128)S(1)} collective-permute-done((f32[6,16,128]{2,1,0:T(8,128)S(1)}, f32[6,16,128]{2,1,0:T(8,128)S(1)}, u32[]{:S(2)}, u32[]{:S(2)}) %collective-permute-start.17) | collective-permute-done | bytes 49184 | tf_op jit(solution)/shard_map/ppermute | solution.py:505
  163.4 1.0 collective-permute-start.24
  164.4 0.1 collective-permute-start.19
  164.5 5.0 %collective-permute-start.21 = (f32[6,32,128]{2,1,0:T(8,128)S(1)}, f32[6,32,128]{2,1,0:T(8,128)S(1)}, u32[]{:S(2)}, u32[]{:S(2)}) collective-permute-start(f32[6,32,128]{2,1,0:T(8,128)S(1)} %constant_dynamic-update-slice_fusion.4.refs_1_), channel_id=1, source_target_pairs={{0,124},{4,0},{8,4},{12,8},{16,12},{20,16},{24,20},{28,24},{32,28}... | collective-permute-start | bytes 294920 | tf_op jit(solution)/shard_map/ppermute | solution.py:505
  169.5 0.7 pad_maximum_fusion.surface
  170.2 9.4 %buildings.2.refs_8_.refs_0_ = f32[1024,256]{1,0:T(8,128)} custom-call(s32[1024]{0:T(1024)} %bitcast.33, s32[1,1024]{1,0:T(1,128)} %bitcast.31, s32[1,1024]{1,0:T(1,128)} %bitcast.29, f32[4,72,128]{2,1,0:T(8,128)} %pad_maximum_fusion.surface, f32[1024,24,128]{2,1,0:T(8,128)} %all-gather.2.cloned.1.call-done.table_ref), custom_call_target="tpu_custom_call" | custom-call | flops 20000000 | bytes 10485760 | tf_op jit(solution)/shard_map/buildings/pallas_call | solution.py:485
  179.6 1.2 copy-done.2
  180.8 11.3 %grid_steps.9 = (f32[768,128]{1,0:T(8,128)}, f32[24,128]{1,0:T(8,128)S(1)}) custom-call(s32[4]{0:T(128)S(1)} %add_convert_fusion.edge, bf16[256,256]{1,0:T(8,128)(2,1)S(1)} %copy-done.3, f32[6,256,128]{2,1,0:T(8,128)} %get-tuple-element.30.refs_0_, f32[6,32,128]{2,1,0:T(8,128)S(1)} %constant_dynamic-update-slice_fusion.4.refs_1_, ...), custom_call_target="tpu_custom_call" | custom-call | flops 40000000 | bytes 8388608 | tf_op jit(solution)/shard_map/grid_steps/pallas_call | solution.py:317
  192.1 1.5 collective-permute-start.25
  193.6 2.0 collective-permute-start.26
  195.6 2.6 %collective-permute-start.27 = (f32[24,128]{1,0:T(8,128)S(1)}, f32[24,128]{1,0:T(8,128)S(1)}, u32[]{:S(2)}, u32[]{:S(2)}) collective-permute-start(f32[24,128]{1,0:T(8,128)S(1)} %get-tuple-element.37), channel_id=1, source_target_pairs={{0,3},{1,0},{2,1},{3,2},{4,7},{5,4},{6,5},{7,6},{8,11},{9,8},{10,9... | collective-permute-start | bytes 36872 | tf_op jit(solution)/shard_map/ppermute | solution.py:505
  198.3 0.6 collective-permute-done.26
  198.8 0.8 collective-permute-done.27
  199.7 0.6 maximum_maximum_fusion.surface
  200.3 6.9 %buildings.3 = f32[1024,256]{1,0:T(8,128)} custom-call(s32[1024]{0:T(1024)} %bitcast.34, s32[1,1024]{1,0:T(1,128)} %bitcast.32, s32[1,1024]{1,0:T(1,128)} %bitcast.30, f32[4,48,128]{2,1,0:T(8,128)} %maximum_maximum_fusion.surface, f32[1024,24,128]{2,1,0:T(8,128)} %all-gather.2.cloned.1.call-done.table_ref, f32[1024,256]{1,0:T(8,128)} %buildings.2.refs_8_.refs_0_), custom_call_target="tpu_custom_call" | custom-call | flops 20000000 | bytes 10485760 | tf_op jit(solution)/shard_map/buildings/pallas_call | solution.py:485
  (44 shorter events, 0.1 us)
Async XLA Ops:
  7.2 163.0 %all-gather.2.cloned.1.call-start = ((), (), s32[]{:S(2)}) async-start(), calls=%async_computation | async-start | bytes 12681216 | tf_op jit(solution)/shard_map/all_gather | solution.py:527
  8.0 1.2 copy-start.4
  9.2 4.2 %copy-start.7 = (f32[3,32,8,128]{3,2,1,0:T(8,128)S(1)}, f32[3,32,8,128]{3,2,1,0:T(8,128)}, u32[]{:S(2)}) copy-start(f32[3,32,8,128]{3,2,1,0:T(8,128)} %param.9) | copy-start | bytes 1179652
  9.2 4.2 %copy-start.8 = (f32[3,32,8,128]{3,2,1,0:T(8,128)S(1)}, f32[3,32,8,128]{3,2,1,0:T(8,128)}, u32[]{:S(2)}) copy-start(f32[3,32,8,128]{3,2,1,0:T(8,128)} %param.10) | copy-start | bytes 1179652
  9.2 4.2 %copy-start.9 = (f32[32,8,128]{2,1,0:T(8,128)S(1)}, f32[32,8,128]{2,1,0:T(8,128)}, u32[]{:S(2)}) copy-start(f32[32,8,128]{2,1,0:T(8,128)} %param.11) | copy-start | bytes 393220
  9.2 4.2 %copy-start.10 = (f32[32,8,128]{2,1,0:T(8,128)S(1)}, f32[32,8,128]{2,1,0:T(8,128)}, u32[]{:S(2)}) copy-start(f32[32,8,128]{2,1,0:T(8,128)} %param.12) | copy-start | bytes 393220
  13.3 24.8 %copy-start.3 = (bf16[256,256]{1,0:T(8,128)(2,1)S(1)}, bf16[256,256]{1,0:T(8,128)(2,1)}, u32[]{:S(2)}) copy-start(bf16[256,256]{1,0:T(8,128)(2,1)} %constant.77.clone.weights_ref) | copy-start | bytes 393220
  14.6 22.6 %collective-permute-start.2 = (f32[8,256,128]{2,1,0:T(8,128)S(1)}, f32[8,256,128]{2,1,0:T(8,128)S(1)}, u32[]{:S(2)}, u32[]{:S(2)}) collective-permute-start(f32[8,256,128]{2,1,0:T(8,128)S(1)} %get-tuple-element.20.refs_0_), channel_id=1, source_target_pairs={{0,4},{4,8},{8,12},{12,16},{16,20},{20,24},{24,28},{28,32},{32,36}... | collective-permute-start | bytes 3145736 | tf_op jit(solution)/shard_map/ppermute | solution.py:505
  14.7 22.5 %collective-permute-start.4 = (f32[8,256,128]{2,1,0:T(8,128)S(1)}, f32[8,256,128]{2,1,0:T(8,128)S(1)}, u32[]{:S(2)}, u32[]{:S(2)}) collective-permute-start(f32[8,256,128]{2,1,0:T(8,128)S(1)} %get-tuple-element.20.refs_0_), channel_id=1, source_target_pairs={{0,124},{4,0},{8,4},{12,8},{16,12},{20,16},{24,20},{28,24},{32,28}... | collective-permute-start | bytes 3145736 | tf_op jit(solution)/shard_map/ppermute | solution.py:505
  20.4 5.0 %collective-permute-start = (f32[8,32,128]{2,1,0:T(8,128)S(1)}, f32[8,32,128]{2,1,0:T(8,128)S(1)}, u32[]{:S(2)}, u32[]{:S(2)}) collective-permute-start(f32[8,32,128]{2,1,0:T(8,128)S(1)} %get-tuple-element.21), channel_id=1, source_target_pairs={{0,1},{1,2},{2,3},{3,0},{4,5},{5,6},{6,7},{7,4},{8,9},{9,10},{10,1... | collective-permute-start | bytes 393224 | tf_op jit(solution)/shard_map/ppermute | solution.py:505
  21.7 5.0 %collective-permute-start.1 = (f32[8,32,128]{2,1,0:T(8,128)S(1)}, f32[8,32,128]{2,1,0:T(8,128)S(1)}, u32[]{:S(2)}, u32[]{:S(2)}) collective-permute-start(f32[8,32,128]{2,1,0:T(8,128)S(1)} %get-tuple-element.22), channel_id=1, source_target_pairs={{0,3},{1,0},{2,1},{3,2},{4,7},{5,4},{6,5},{7,6},{8,11},{9,8},{10,9... | collective-permute-start | bytes 393224 | tf_op jit(solution)/shard_map/ppermute | solution.py:505
  27.3 9.8 %collective-permute-start.3 = (f32[8,64,128]{2,1,0:T(8,128)}, f32[8,64,128]{2,1,0:T(8,128)}, u32[]{:S(2)}, u32[]{:S(2)}) collective-permute-start(f32[8,64,128]{2,1,0:T(8,128)} %constant_dynamic-update-slice_fusion.refs_1_), channel_id=1, source_target_pairs={{0,4},{4,8},{8,12},{12,16},{16,20},{20,24},{24,28},{28,32},{32,36}... | collective-permute-start | bytes 786440 | tf_op jit(solution)/shard_map/ppermute | solution.py:505
  27.3 9.8 %collective-permute-start.5 = (f32[8,64,128]{2,1,0:T(8,128)}, f32[8,64,128]{2,1,0:T(8,128)}, u32[]{:S(2)}, u32[]{:S(2)}) collective-permute-start(f32[8,64,128]{2,1,0:T(8,128)} %constant_dynamic-update-slice_fusion.refs_1_), channel_id=1, source_target_pairs={{0,124},{4,0},{8,4},{12,8},{16,12},{20,16},{24,20},{28,24},{32,28}... | collective-permute-start | bytes 786440 | tf_op jit(solution)/shard_map/ppermute | solution.py:505
  37.2 1.0 copy-start.5
  38.1 1.2 copy-start.6
  52.7 17.2 %collective-permute-start.6 = (f32[6,288,128]{2,1,0:T(8,128)S(1)}, f32[6,288,128]{2,1,0:T(8,128)S(1)}, u32[]{:S(2)}, u32[]{:S(2)}) collective-permute-start(f32[6,288,128]{2,1,0:T(8,128)S(1)} %get-tuple-element.23.refs_0_), channel_id=1, source_target_pairs={{0,4},{4,8},{8,12},{12,16},{16,20},{20,24},{24,28},{28,32},{32,36}... | collective-permute-start | bytes 2654216 | tf_op jit(solution)/shard_map/ppermute | solution.py:505
  52.7 17.2 %collective-permute-start.7 = (f32[6,288,128]{2,1,0:T(8,128)S(1)}, f32[6,288,128]{2,1,0:T(8,128)S(1)}, u32[]{:S(2)}, u32[]{:S(2)}) collective-permute-start(f32[6,288,128]{2,1,0:T(8,128)S(1)} %get-tuple-element.23.refs_0_), channel_id=1, source_target_pairs={{0,124},{4,0},{8,4},{12,8},{16,12},{20,16},{24,20},{28,24},{32,28}... | collective-permute-start | bytes 2654216 | tf_op jit(solution)/shard_map/ppermute | solution.py:505
  69.9 1.3 copy-start
  80.8 29.3 %collective-permute-start.10 = (f32[6,256,128]{2,1,0:T(8,128)S(1)}, f32[6,256,128]{2,1,0:T(8,128)S(1)}, u32[]{:S(2)}, u32[]{:S(2)}) collective-permute-start(f32[6,256,128]{2,1,0:T(8,128)S(1)} %get-tuple-element.26.refs_0_), channel_id=1, source_target_pairs={{0,4},{4,8},{8,12},{12,16},{16,20},{20,24},{24,28},{28,32},{32,36}... | collective-permute-start | bytes 2359304 | tf_op jit(solution)/shard_map/ppermute | solution.py:505
  80.8 29.2 %collective-permute-start.12 = (f32[6,256,128]{2,1,0:T(8,128)S(1)}, f32[6,256,128]{2,1,0:T(8,128)S(1)}, u32[]{:S(2)}, u32[]{:S(2)}) collective-permute-start(f32[6,256,128]{2,1,0:T(8,128)S(1)} %get-tuple-element.26.refs_0_), channel_id=1, source_target_pairs={{0,124},{4,0},{8,4},{12,8},{16,12},{20,16},{24,20},{28,24},{32,28}... | collective-permute-start | bytes 2359304 | tf_op jit(solution)/shard_map/ppermute | solution.py:505
  85.9 5.9 %collective-permute-start.8 = (f32[6,32,128]{2,1,0:T(8,128)S(1)}, f32[6,32,128]{2,1,0:T(8,128)S(1)}, u32[]{:S(2)}, u32[]{:S(2)}) collective-permute-start(f32[6,32,128]{2,1,0:T(8,128)S(1)} %get-tuple-element.27), channel_id=1, source_target_pairs={{0,1},{1,2},{2,3},{3,0},{4,5},{5,6},{6,7},{7,4},{8,9},{9,10},{10,1... | collective-permute-start | bytes 294920 | tf_op jit(solution)/shard_map/ppermute | solution.py:505
  87.3 6.0 %collective-permute-start.9 = (f32[6,32,128]{2,1,0:T(8,128)S(1)}, f32[6,32,128]{2,1,0:T(8,128)S(1)}, u32[]{:S(2)}, u32[]{:S(2)}) collective-permute-start(f32[6,32,128]{2,1,0:T(8,128)S(1)} %get-tuple-element.28), channel_id=1, source_target_pairs={{0,3},{1,0},{2,1},{3,2},{4,7},{5,4},{6,5},{7,6},{8,11},{9,8},{10,9... | collective-permute-start | bytes 294920 | tf_op jit(solution)/shard_map/ppermute | solution.py:505
  93.3 45.1 %copy-start.1 = (f32[28,80,128]{2,1,0:T(8,128)S(1)}, f32[28,80,128]{2,1,0:T(8,128)}, u32[]{:S(2)}) copy-start(f32[28,80,128]{2,1,0:T(8,128)} %get-tuple-element.25.refs_4_.refs_7_) | copy-start | bytes 3440644
  93.3 16.7 %collective-permute-start.11 = (f32[6,64,128]{2,1,0:T(8,128)S(1)}, f32[6,64,128]{2,1,0:T(8,128)S(1)}, u32[]{:S(2)}, u32[]{:S(2)}) collective-permute-start(f32[6,64,128]{2,1,0:T(8,128)S(1)} %constant_dynamic-update-slice_fusion.2.refs_1_), channel_id=1, source_target_pairs={{0,4},{4,8},{8,12},{12,16},{16,20},{20,24},{24,28},{28,32},{32,36}... | collective-permute-start | bytes 589832 | tf_op jit(solution)/shard_map/ppermute | solution.py:505
  93.4 16.6 %collective-permute-start.13 = (f32[6,64,128]{2,1,0:T(8,128)S(1)}, f32[6,64,128]{2,1,0:T(8,128)S(1)}, u32[]{:S(2)}, u32[]{:S(2)}) collective-permute-start(f32[6,64,128]{2,1,0:T(8,128)S(1)} %constant_dynamic-update-slice_fusion.2.refs_1_), channel_id=1, source_target_pairs={{0,124},{4,0},{8,4},{12,8},{16,12},{20,16},{24,20},{28,24},{32,28}... | collective-permute-start | bytes 589832 | tf_op jit(solution)/shard_map/ppermute | solution.py:505
  122.4 16.0 %collective-permute-start.14 = (f32[6,288,128]{2,1,0:T(8,128)S(1)}, f32[6,288,128]{2,1,0:T(8,128)}, u32[]{:S(2)}, u32[]{:S(2)}) collective-permute-start(f32[6,288,128]{2,1,0:T(8,128)S(1)} %get-tuple-element.29.refs_0_), channel_id=1, source_target_pairs={{0,4},{4,8},{8,12},{12,16},{16,20},{20,24},{24,28},{28,32},{32,36}... | collective-permute-start | bytes 2654216 | tf_op jit(solution)/shard_map/ppermute | solution.py:505
  122.5 15.9 %collective-permute-start.15 = (f32[6,288,128]{2,1,0:T(8,128)S(1)}, f32[6,288,128]{2,1,0:T(8,128)}, u32[]{:S(2)}, u32[]{:S(2)}) collective-permute-start(f32[6,288,128]{2,1,0:T(8,128)S(1)} %get-tuple-element.29.refs_0_), channel_id=1, source_target_pairs={{0,124},{4,0},{8,4},{12,8},{16,12},{20,16},{24,20},{28,24},{32,28}... | collective-permute-start | bytes 2654216 | tf_op jit(solution)/shard_map/ppermute | solution.py:505
  127.5 27.1 %copy-start.11 = (s32[1024]{0:T(1024)S(1)}, s32[1024]{0:T(1024)}, u32[]{:S(2)}) copy-start(s32[1024]{0:T(1024)} %param.13) | copy-start | bytes 12292
  149.5 30.1 %collective-permute-start.18 = (f32[6,256,128]{2,1,0:T(8,128)}, f32[6,256,128]{2,1,0:T(8,128)S(1)}, u32[]{:S(2)}, u32[]{:S(2)}) collective-permute-start(f32[6,256,128]{2,1,0:T(8,128)} %get-tuple-element.30.refs_0_), channel_id=1, source_target_pairs={{0,4},{4,8},{8,12},{12,16},{16,20},{20,24},{24,28},{28,32},{32,36}... | collective-permute-start | bytes 2359304 | tf_op jit(solution)/shard_map/ppermute | solution.py:505
  149.5 30.1 %collective-permute-start.20 = (f32[6,256,128]{2,1,0:T(8,128)}, f32[6,256,128]{2,1,0:T(8,128)}, u32[]{:S(2)}, u32[]{:S(2)}) collective-permute-start(f32[6,256,128]{2,1,0:T(8,128)} %get-tuple-element.30.refs_0_), channel_id=1, source_target_pairs={{0,124},{4,0},{8,4},{12,8},{16,12},{20,16},{24,20},{28,24},{32,28}... | collective-permute-start | bytes 2359304 | tf_op jit(solution)/shard_map/ppermute | solution.py:505
  155.2 4.1 %collective-permute-start.16 = (f32[6,16,128]{2,1,0:T(8,128)S(1)}, f32[6,16,128]{2,1,0:T(8,128)S(1)}, u32[]{:S(2)}, u32[]{:S(2)}) collective-permute-start(f32[6,16,128]{2,1,0:T(8,128)S(1)} %get-tuple-element.31), channel_id=1, source_target_pairs={{0,1},{1,2},{2,3},{3,0},{4,5},{5,6},{6,7},{7,4},{8,9},{9,10},{10,1... | collective-permute-start | bytes 147464 | tf_op jit(solution)/shard_map/ppermute | solution.py:505
  156.4 8.0 %collective-permute-start.22 = (f32[72,128]{1,0:T(8,128)S(1)}, f32[72,128]{1,0:T(8,128)S(1)}, u32[]{:S(2)}, u32[]{:S(2)}) collective-permute-start(f32[72,128]{1,0:T(8,128)S(1)} %constant_dynamic-update-slice_fusion.6), channel_id=1, source_target_pairs={{0,1},{1,2},{2,3},{3,0},{4,5},{5,6},{6,7},{7,4},{8,9},{9,10},{10,1... | collective-permute-start | bytes 110600 | tf_op jit(solution)/shard_map/ppermute | solution.py:505
  156.9 7.5 %collective-permute-start.23 = (f32[72,128]{1,0:T(8,128)S(1)}, f32[72,128]{1,0:T(8,128)S(1)}, u32[]{:S(2)}, u32[]{:S(2)}) collective-permute-start(f32[72,128]{1,0:T(8,128)S(1)} %constant_dynamic-update-slice_fusion.6), channel_id=1, source_target_pairs={{0,2},{1,3},{2,0},{3,1},{4,6},{5,7},{6,4},{7,5},{8,10},{9,11},{10,... | collective-permute-start | bytes 110600 | tf_op jit(solution)/shard_map/ppermute | solution.py:505
  159.3 4.1 %collective-permute-start.17 = (f32[6,16,128]{2,1,0:T(8,128)S(1)}, f32[6,16,128]{2,1,0:T(8,128)S(1)}, u32[]{:S(2)}, u32[]{:S(2)}) collective-permute-start(f32[6,16,128]{2,1,0:T(8,128)S(1)} %get-tuple-element.32), channel_id=1, source_target_pairs={{0,3},{1,0},{2,1},{3,2},{4,7},{5,4},{6,5},{7,6},{8,11},{9,8},{10,9... | collective-permute-start | bytes 147464 | tf_op jit(solution)/shard_map/ppermute | solution.py:505
  163.4 6.1 %collective-permute-start.24 = (f32[72,128]{1,0:T(8,128)S(1)}, f32[72,128]{1,0:T(8,128)S(1)}, u32[]{:S(2)}, u32[]{:S(2)}) collective-permute-start(f32[72,128]{1,0:T(8,128)S(1)} %constant_dynamic-update-slice_fusion.6), channel_id=1, source_target_pairs={{0,3},{1,0},{2,1},{3,2},{4,7},{5,4},{6,5},{7,6},{8,11},{9,8},{10,9... | collective-permute-start | bytes 110600 | tf_op jit(solution)/shard_map/ppermute | solution.py:505
  164.4 15.2 %collective-permute-start.19 = (f32[6,32,128]{2,1,0:T(8,128)S(1)}, f32[6,32,128]{2,1,0:T(8,128)S(1)}, u32[]{:S(2)}, u32[]{:S(2)}) collective-permute-start(f32[6,32,128]{2,1,0:T(8,128)S(1)} %constant_dynamic-update-slice_fusion.4.refs_1_), channel_id=1, source_target_pairs={{0,4},{4,8},{8,12},{12,16},{16,20},{20,24},{24,28},{28,32},{32,36}... | collective-permute-start | bytes 294920 | tf_op jit(solution)/shard_map/ppermute | solution.py:505
  164.5 15.1 %collective-permute-start.21 = (f32[6,32,128]{2,1,0:T(8,128)S(1)}, f32[6,32,128]{2,1,0:T(8,128)S(1)}, u32[]{:S(2)}, u32[]{:S(2)}) collective-permute-start(f32[6,32,128]{2,1,0:T(8,128)S(1)} %constant_dynamic-update-slice_fusion.4.refs_1_), channel_id=1, source_target_pairs={{0,124},{4,0},{8,4},{12,8},{16,12},{20,16},{24,20},{28,24},{32,28}... | collective-permute-start | bytes 294920 | tf_op jit(solution)/shard_map/ppermute | solution.py:505
  170.2 29.5 %slice-start = ((f32[4,72,128]{2,1,0:T(8,128)}), f32[4,24,128]{2,1,0:T(8,128)S(1)}, s32[]{:S(2)}) async-start(f32[4,72,128]{2,1,0:T(8,128)} %pad_maximum_fusion.surface), calls=%async_computation.1 | async-start | bytes 98304 | tf_op jit(solution)/shard_map/slice | solution.py:562
  179.6 1.2 copy-start.2
  192.1 6.2 %collective-permute-start.25 = (f32[24,128]{1,0:T(8,128)S(1)}, f32[24,128]{1,0:T(8,128)S(1)}, u32[]{:S(2)}, u32[]{:S(2)}) collective-permute-start(f32[24,128]{1,0:T(8,128)S(1)} %get-tuple-element.37), channel_id=1, source_target_pairs={{0,1},{1,2},{2,3},{3,0},{4,5},{5,6},{6,7},{7,4},{8,9},{9,10},{10,1... | collective-permute-start | bytes 36872 | tf_op jit(solution)/shard_map/ppermute | solution.py:505
  193.6 5.2 %collective-permute-start.26 = (f32[24,128]{1,0:T(8,128)S(1)}, f32[24,128]{1,0:T(8,128)S(1)}, u32[]{:S(2)}, u32[]{:S(2)}) collective-permute-start(f32[24,128]{1,0:T(8,128)S(1)} %get-tuple-element.37), channel_id=1, source_target_pairs={{0,2},{1,3},{2,0},{3,1},{4,6},{5,7},{6,4},{7,5},{8,10},{9,11},{10,... | collective-permute-start | bytes 36872 | tf_op jit(solution)/shard_map/ppermute | solution.py:505
  195.6 4.0 %collective-permute-start.27 = (f32[24,128]{1,0:T(8,128)S(1)}, f32[24,128]{1,0:T(8,128)S(1)}, u32[]{:S(2)}, u32[]{:S(2)}) collective-permute-start(f32[24,128]{1,0:T(8,128)S(1)} %get-tuple-element.37), channel_id=1, source_target_pairs={{0,3},{1,0},{2,1},{3,2},{4,7},{5,4},{6,5},{7,6},{8,11},{9,8},{10,9... | collective-permute-start | bytes 36872 | tf_op jit(solution)/shard_map/ppermute | solution.py:505
Sparse Core Ops, SparseCore 0:
  13.5 92.4 all-gather.1
